TPU v7x, 32 devices: a whole 2x2x4 slice. The times are simulated.
32 devices in a mesh: groups: 2 (over x), store: 4 (over y, core), tensor: 4 (over z).
Axes of the slice: x: 2, y: 2, z: 4, core: 2. Of those that a mesh axis runs over, the one named last changes fastest.
Arguments:
- queries: bfloat16 [16384, 4096], P(('groups', 'store'), 'tensor'), parts along dimension 0, may hold values from -6 to 6
- suffix_cache: bfloat16 [16384, 2, 1024], P(('groups', 'store'), None, 'tensor'), parts along dimension 0, may hold values from -5 to 5
- cache_blocks: bfloat16 [128, 2, 128, 1024], P(('groups', 'store'), None, None, 'tensor'), parts along dimension 0, may hold values from -6 to 6
- cache_states: bfloat16 [32, 4096, 128], P(('groups', 'store'), 'tensor'), parts along dimension 0, may hold values from -5 to 5
- ssm_input: bfloat16 [16384, 4096], P(('groups', 'store'), 'tensor'), parts along dimension 0, may hold values from -60 to 60
- gate_input: bfloat16 [16384, 4096], P(('groups', 'store'), 'tensor'), parts along dimension 0, may hold values from -5 to 5
- state_maps: bfloat16 [16384, 2, 128], P(('groups', 'store')), parts along dimension 0, may hold values from -1.5 to 1.5
- step_size: float32 [128, 8192], P(('groups', 'tensor'), 'store'), parts along dimension 0, may hold values from 0 to 0.4
- decay_log: float32 [64], P('tensor'), may hold values from -0.5 to 0.5
- skip: float32 [64], P('tensor'), may hold values from 0.5 to 12
- norm_gain: float32 [4096], P('tensor'), may hold values from 0.1 to 1.9
- hit_owner: int32 [32, 8, 1], P('groups'), parts along dimension 0, may hold values from 0 to 3; in each aligned block of 32 rows (0 to 31, 32 to 63, ..., all dimensions but the last counted through in order) at most 16 rows name the same one
- hit_block: int32 [32, 8], P('groups'), parts along dimension 0, may hold values from 0 to 15
- hit_len: int32 [32], P('groups'), parts along dimension 0, may hold values from 1 to 8, 112 in all
- saved_owner: int32 [32, 1], P('groups'), parts along dimension 0, may hold values from 0 to 3; in each aligned block of 4 rows (0 to 3, 4 to 7, ...) at most 2 rows name the same one
- saved_slot: int32 [32], P('groups'), parts along dimension 0, may hold values from 0 to 3
Outputs:
- attn_out: bfloat16 [16384, 4096], P(('groups', 'store'), 'tensor'), parts along dimension 0
- ssm_out: bfloat16 [16384, 4096], P(('groups', 'store'), 'tensor'), parts along dimension 0
- final_state: float32 [32, 4096, 128], P(('groups', 'store'), 'tensor'), parts along dimension 0
There are 2 independent parts, one for each index of `groups`. A program takes and returns all parts, laid end to end along the dimension named above; an argument that names none is the same for every part. Nothing has to cross between parts.
Inputs may be any that keep to these rules, and one draw needn't show every extreme that they name: `hit_owner`: among the 32 entries of the 4 requests of one store index, no owner is named more than 16 times, a bound that some block reaches. `hit_len`: the longest match is exactly 8 blocks. `saved_owner`: among the 4 requests of one store index, no owner holds more than 2 of their checkpoints, a bound that some block reaches.
All inputs are finite; a program needn't handle non-finite values.
Results may differ from a plain program's by a relative error of at most 0.0046.
Values may be sent and summed in bfloat16 or wider, within the bound.
A program may use at most 128 MiB of HBM per device.

v0:
```python
import jax
import jax.numpy as jnp
from jax import lax
from jax.sharding import PartitionSpec as P

HEAD_DIM = 128
SSM_DIM = 64
STRETCH = 128
REQUEST_NEW = 512


def stretch_scan(inputs, in_maps, out_maps, steps, rates, start_state):
    length, channels = inputs.shape
    head_count = steps.shape[0]
    head_width = channels // head_count
    blocks = length // STRETCH
    highest = lax.Precision.HIGHEST
    input_blocks = inputs.reshape(blocks, STRETCH, channels)
    in_blocks = in_maps.reshape(blocks, STRETCH, -1)
    out_blocks = out_maps.reshape(blocks, STRETCH, -1)
    step_blocks = steps.reshape(head_count, blocks, STRETCH).transpose(1, 0, 2)
    causal = jnp.arange(STRETCH)[:, None] >= jnp.arange(STRETCH)[None, :]

    def advance(state, piece_list):
        block_flat, map_in, map_out, block_steps = piece_list
        block_in = block_flat.reshape(STRETCH, head_count, head_width)
        running = jnp.cumsum(block_steps * rates[:, None], axis=1)
        spans = jnp.where(causal[None], running[:, :, None] - running[:, None, :], -jnp.inf)
        intersections = jnp.dot(map_out, map_in.T, preferred_element_type=jnp.float32)
        map_in_wide = map_in.astype(jnp.float32)
        map_out_wide = map_out.astype(jnp.float32)
        mixing = jnp.exp(spans) * intersections[None] * block_steps[:, None, :]
        within = jnp.einsum("hij,jhp->ihp", mixing, block_in, precision=highest)
        carried = (
            jnp.einsum("in,hpn->ihp", map_out_wide, state, precision=highest)
            * jnp.exp(running).T[:, :, None]
        )
        remaining = (jnp.exp(running[:, -1:] - running) * block_steps).T
        update = jnp.einsum(
            "jhp,jn->hpn", remaining[:, :, None] * block_in, map_in_wide, precision=highest
        )
        new_state = jnp.exp(running[:, -1])[:, None, None] * state + update
        return (new_state, (within + carried).reshape(STRETCH, channels))

    last_state, results = lax.scan(
        advance, start_state, (input_blocks, in_blocks, out_blocks, step_blocks)
    )
    return (results.reshape(length, channels), last_state)


def owner_rank(owners, stores):
    onehot = (owners[:, :, None] == jnp.arange(stores)[None, None, :]).astype(jnp.int32)
    before = jnp.cumsum(onehot, axis=1) - onehot
    return jnp.sum(before * onehot, axis=2)


def pack_slots(source, owners, ranks, numbers, alive, position, slots):
    chosen = (owners == position) & alive
    select = chosen[:, None, :] & (ranks[:, None, :] == jnp.arange(slots)[None, :, None])
    picked = jnp.sum(jnp.where(select, numbers[:, None, :], 0), axis=2)
    filled = jnp.any(select, axis=2).reshape((-1,) + (1,) * (source.ndim - 1))
    taken = jnp.take(source, picked.reshape(-1), axis=0)
    taken = jnp.where(filled, taken, jnp.zeros((), source.dtype))
    return taken.reshape((owners.shape[0], slots) + source.shape[1:])


def unpack_slots(arrived, my_owner, my_rank, slots):
    flat = arrived.reshape((-1,) + arrived.shape[2:])
    return jnp.take(flat, my_owner * slots + my_rank, axis=0)


def body(
    queries,
    suffix_cache,
    cache_blocks,
    cache_states,
    ssm_input,
    gate_input,
    state_maps,
    step_size,
    decay_log,
    skip,
    norm_gain,
    hit_owner,
    hit_block,
    hit_len,
    saved_owner,
    saved_slot,
):
    stores = lax.axis_size("store")
    position = lax.axis_index("store")
    requests = queries.shape[0] // REQUEST_NEW
    max_blocks = hit_block.shape[1]
    block_rows = cache_blocks.shape[2]
    per_device = requests * max_blocks
    owners = hit_owner[:, :, 0].reshape(stores, per_device)
    numbers = hit_block.reshape(stores, per_device)
    alive = (jnp.arange(max_blocks)[None, :] < hit_len[:, None]).reshape(stores, per_device)
    my_owner = lax.dynamic_index_in_dim(owners, position, 0, keepdims=False)
    slots = max(2, 2 * per_device // stores)
    ranks = owner_rank(owners, stores)
    outgoing = pack_slots(cache_blocks, owners, ranks, numbers, alive, position, slots)
    arrived = lax.all_to_all(outgoing, "store", split_axis=0, concat_axis=0, tiled=True)
    my_rank = lax.dynamic_index_in_dim(ranks, position, 0, keepdims=False)
    prefix = unpack_slots(arrived, my_owner, my_rank, slots)
    state_owners = saved_owner[:, 0].reshape(stores, requests)
    state_numbers = saved_slot.reshape(stores, requests)
    state_alive = jnp.ones((stores, requests), dtype=bool)
    my_state_owner = lax.dynamic_index_in_dim(state_owners, position, 0, keepdims=False)
    state_slots = max(2, 2 * requests // stores)
    state_ranks = owner_rank(state_owners, stores)
    outgoing_states = pack_slots(
        cache_states, state_owners, state_ranks, state_numbers, state_alive, position, state_slots
    )
    arrived_states = lax.all_to_all(
        outgoing_states, "store", split_axis=0, concat_axis=0, tiled=True
    )
    my_state_rank = lax.dynamic_index_in_dim(state_ranks, position, 0, keepdims=False)
    saved = unpack_slots(arrived_states, my_state_owner, my_state_rank, state_slots)
    kv_width = cache_blocks.shape[3]
    key_value_rows = kv_width // HEAD_DIM
    q_local = queries.shape[1] // HEAD_DIM
    group = q_local // key_value_rows
    prefix_rows = max_blocks * block_rows
    scale = HEAD_DIM ** (-0.5)
    query_all = queries.reshape(requests, REQUEST_NEW, key_value_rows, group, HEAD_DIM)
    prefix_all = prefix.reshape(requests, max_blocks, 2, block_rows, kv_width)
    fresh_all = suffix_cache.reshape(requests, REQUEST_NEW, 2, kv_width)
    my_lengths = lax.dynamic_slice_in_dim(hit_len, position * requests, requests, 0)
    prefix_place = jnp.arange(prefix_rows) // block_rows
    asker_position = jnp.arange(REQUEST_NEW)
    fresh_visible = asker_position[None, :] <= asker_position[:, None]

    def attend(index):
        query_rows = lax.dynamic_index_in_dim(query_all, index, 0, keepdims=False)
        stored = lax.dynamic_index_in_dim(prefix_all, index, 0, keepdims=False)
        fresh = lax.dynamic_index_in_dim(fresh_all, index, 0, keepdims=False)
        matched = lax.dynamic_index_in_dim(my_lengths, index, 0, keepdims=False)
        old_keys = stored[:, 0].reshape(prefix_rows, key_value_rows, HEAD_DIM)
        old_values = stored[:, 1].reshape(prefix_rows, key_value_rows, HEAD_DIM)
        new_keys = fresh[:, 0].reshape(REQUEST_NEW, key_value_rows, HEAD_DIM)
        new_values = fresh[:, 1].reshape(REQUEST_NEW, key_value_rows, HEAD_DIM)
        old_scores = (
            jnp.einsum("ikgd,jkd->kgij", query_rows, old_keys, preferred_element_type=jnp.float32)
            * scale
        )
        new_scores = (
            jnp.einsum("ikgd,jkd->kgij", query_rows, new_keys, preferred_element_type=jnp.float32)
            * scale
        )
        old_visible = (prefix_place < matched)[None, :]
        old_masked = jnp.where(old_visible, old_scores, -jnp.inf)
        new_masked = jnp.where(fresh_visible, new_scores, -jnp.inf)
        peak = jnp.maximum(
            jnp.max(old_masked, axis=-1, keepdims=True), jnp.max(new_masked, axis=-1, keepdims=True)
        )
        old_weights = jnp.exp(old_masked - peak)
        new_weights = jnp.exp(new_masked - peak)
        total = jnp.sum(old_weights, axis=-1) + jnp.sum(new_weights, axis=-1)
        mixed_heads = jnp.einsum(
            "kgij,jkd->ikgd",
            old_weights.astype(jnp.bfloat16),
            old_values,
            preferred_element_type=jnp.float32,
        )
        mixed_heads = mixed_heads + jnp.einsum(
            "kgij,jkd->ikgd",
            new_weights.astype(jnp.bfloat16),
            new_values,
            preferred_element_type=jnp.float32,
        )
        result = mixed_heads / total.transpose(2, 0, 1)[..., None]
        return result.astype(jnp.bfloat16).reshape(REQUEST_NEW, q_local * HEAD_DIM)

    request_ids = jnp.arange(requests, dtype=jnp.int32)
    attn_out = lax.map(attend, request_ids).reshape(requests * REQUEST_NEW, q_local * HEAD_DIM)
    heads_local = ssm_input.shape[1] // SSM_DIM
    channels_local = heads_local * SSM_DIM
    rates = -jnp.exp(decay_log)
    skip_wide = jnp.repeat(skip, SSM_DIM)

    def mamba(index):
        first = index * REQUEST_NEW
        inputs = lax.dynamic_slice_in_dim(ssm_input, first, REQUEST_NEW, 0).astype(jnp.float32)
        maps = lax.dynamic_slice_in_dim(state_maps, first, REQUEST_NEW, 0)
        steps = lax.dynamic_slice_in_dim(step_size, first, REQUEST_NEW, 1)
        start_state = lax.dynamic_index_in_dim(saved, index, 0, keepdims=False).astype(jnp.float32)
        start_state = start_state.reshape(heads_local, SSM_DIM, -1)
        outputs, last_state = stretch_scan(
            inputs, maps[:, 0], maps[:, 1], steps, rates, start_state
        )
        outputs = outputs + skip_wide[None, :] * inputs
        return (outputs, last_state.reshape(channels_local, -1))

    outputs, final_state = lax.map(mamba, request_ids)
    mixed = outputs.reshape(requests * REQUEST_NEW, channels_local) * jax.nn.silu(
        gate_input.astype(jnp.float32)
    )
    squares = lax.psum(jnp.sum(mixed * mixed, axis=1), "tensor")
    channels = channels_local * lax.axis_size("tensor")
    ssm_out = (mixed * lax.rsqrt(squares / channels + 1e-05)[:, None] * norm_gain).astype(
        jnp.bfloat16
    )
    return (attn_out, ssm_out, final_state)


def solution(mesh):
    in_specs = (
        P(("groups", "store"), "tensor"),
        P(("groups", "store"), None, "tensor"),
        P(("groups", "store"), None, None, "tensor"),
        P(("groups", "store"), "tensor", None),
        P(("groups", "store"), "tensor"),
        P(("groups", "store"), "tensor"),
        P(("groups", "store"), None, None),
        P(("groups", "tensor"), "store"),
        P("tensor"),
        P("tensor"),
        P("tensor"),
        P("groups", None, None),
        P("groups", None),
        P("groups"),
        P("groups", None),
        P("groups"),
    )
    out_specs = (
        P(("groups", "store"), "tensor"),
        P(("groups", "store"), "tensor"),
        P(("groups", "store"), "tensor", None),
    )
    return jax.shard_map(body, mesh=mesh, in_specs=in_specs, out_specs=out_specs, check_vma=False)
```

profile of v0, /device:TPU:0, one launch (start us, length us, event | category | flops | bytes accessed | tf_op | source)
XLA Modules:
  0.0 425.9 jit_solution(1094452171589184166)
XLA Ops:
  17.9 7.8 %reshape.297 = bf16[4,512,2,4,128]{4,3,2,1,0:T(4,128)(2,1)} reshape(bf16[2048,1024]{1,0:T(8,128)(2,1)} %param.22) | data formatting | bytes 8388608 | tf_op jit(solution)/shard_map/reshape | solution.py:126
  31.2 7.6 %select_select_fusion = bf16[4,16,2,128,256]{4,3,2,1,0:T(8,128)(2,1)} fusion(bf16[4,16,2,128,256]{4,3,2,1,0:T(8,128)(2,1)} %bitcast.243, pred[4,16]{1,0:T(4,128)(4,1)S(1)} %compare_and_fusion.2, pred[4,16]{1,0:T(4,128)(4,1)S(1)} %fusion.66), kind=kLoop, calls=%fused_computation.101 | loop fusion | flops 8388608 | bytes 16777344 | tf_op jit(solution)/shard_map/jit(_where)/select_n | solution.py:63
  51.1 154.8 %while.40 = (s32[]{:T(128)}, f32[4,512,1024]{2,1,0:T(8,128)}, f32[4,1024,128]{2,1,0:T(8,128)}, s32[4]{0:T(128)S(1)}, bf16[4,1024,128]{2,1,0:T(8,128)(2,1)}, /*in...) while((s32[]{:T(128)}, f32[4,512,1024]{2,1,0:T(8,128)}, ...), condition=%wide.region_18.19_spmd.clone, body=%wide.region_14.18_spmd.clone.sunk | while | flops 612388864 | bytes 21793232 | solution.py:195
  59.6 25.7 %while.41 = (s32[]{:T(128)}, f32[16,64,128]{2,1,0:T(8,128)S(1)}, f32[4,128,1024]{2,1,0:T(8,128)}, f32[4,16,128]{2,0,1:T(4,128)S(1)}, f32[16]{0:T(128)S(1)}, /*in...) while((s32[]{:T(128)}, f32[16,64,128]{2,1,0:T(8,128)S(1)}, ...), condition=%wide.region_17.17_spmd.clone, body=%wide.region_15.16_spmd.clone.sunk | while | flops 610160640 | bytes 9848837 | solution.py:45
  98.3 25.7 %while.41 = (s32[]{:T(128)}, f32[16,64,128]{2,1,0:T(8,128)S(1)}, f32[4,128,1024]{2,1,0:T(8,128)}, f32[4,16,128]{2,0,1:T(4,128)S(1)}, f32[16]{0:T(128)S(1)}, /*in...) while((s32[]{:T(128)}, f32[16,64,128]{2,1,0:T(8,128)S(1)}, ...), condition=%wide.region_17.17_spmd.clone, body=%wide.region_15.16_spmd.clone.sunk | while | flops 610160640 | bytes 9848837 | solution.py:45
  137.0 25.7 %while.41 = (s32[]{:T(128)}, f32[16,64,128]{2,1,0:T(8,128)S(1)}, f32[4,128,1024]{2,1,0:T(8,128)}, f32[4,16,128]{2,0,1:T(4,128)S(1)}, f32[16]{0:T(128)S(1)}, /*in...) while((s32[]{:T(128)}, f32[16,64,128]{2,1,0:T(8,128)S(1)}, ...), condition=%wide.region_17.17_spmd.clone, body=%wide.region_15.16_spmd.clone.sunk | while | flops 610160640 | bytes 9848837 | solution.py:45
  175.7 25.7 %while.41 = (s32[]{:T(128)}, f32[16,64,128]{2,1,0:T(8,128)S(1)}, f32[4,128,1024]{2,1,0:T(8,128)}, f32[4,16,128]{2,0,1:T(4,128)S(1)}, f32[16]{0:T(128)S(1)}, /*in...) while((s32[]{:T(128)}, f32[16,64,128]{2,1,0:T(8,128)S(1)}, ...), condition=%wide.region_17.17_spmd.clone, body=%wide.region_15.16_spmd.clone.sunk | while | flops 610160640 | bytes 9848837 | solution.py:45
  205.9 5.9 %multiply_reduce_fusion = f32[2048]{0:T(1024)S(1)} fusion(bf16[2048,1024]{1,0:T(8,128)(2,1)} %param.27, f32[4,512,1024]{2,1,0:T(8,128)} %get-tuple-element.152), kind=kLoop, calls=%fused_computation.100 | loop fusion | flops 16775168 | bytes 12591104 | tf_op jit(solution)/shard_map/reduce_sum | solution.py:199
  211.9 13.0 %psum.7 = f32[2048]{0:T(1024)S(1)} all-reduce(f32[2048]{0:T(1024)S(1)} %multiply_reduce_fusion), channel_id=1, replica_groups=mesh['groups'=2,'store'=4,'tensor'=4] {'tensor'}, use_global_device_ids=true, to_apply=%region_20.21 | all-reduce | flops 2048 | bytes 16384 | tf_op jit(solution)/shard_map/psum | solution.py:199
  224.9 7.4 %multiply_convert_fusion = bf16[2048,1024]{1,0:T(8,128)(2,1)} fusion(f32[1024]{0:T(1024)S(1)} %copy-done.5, f32[2048]{0:T(1024)S(1)} %add_rsqrt_fusion, bf16[2048,1024]{1,0:T(8,128)(2,1)} %param.27, f32[4,512,1024]{2,1,0:T(8,128)} %get-tuple-element.152), kind=kLoop, calls=%fused_computation.99 | loop fusion | flops 18874368 | bytes 16789504 | tf_op jit(solution)/shard_map/convert_element_type | solution.py:201
  232.3 6.2 %gather_fusion.1 = bf16[32,2,128,256]{3,2,1,0:T(8,128)(2,1)} fusion(bf16[64,2,128,256]{3,2,1,0:T(8,128)(2,1)} %bitcast.2, s32[1024]{0:T(1024)S(1)} %pad_clamp_fusion.2), kind=kCustom, calls=%fused_computation.1 | custom fusion | bytes 8388736 | tf_op jit(solution)/shard_map/jit(_take)/gather | solution.py:69
  243.0 181.2 %while.38 = (s32[]{:T(128)}, bf16[4,512,1024]{2,1,0:T(8,128)(2,1)}, s32[4]{0:T(128)S(1)}, bf16[4,8,2,128,256]{4,3,2,1,0:T(8,128)(2,1)}, s32[4]{0:T(128)S(1)}, /*...) while((s32[]{:T(128)}, bf16[4,512,1024]{2,1,0:T(8,128)(2,1)}, ...), condition=%wide.region_9.10_spmd.clone, body=%wide.region_4.9_spmd.clone.sunk | while | flops 3292267520 | bytes 137089248 | solution.py:176
  251.1 7.7 %bitcast_reduce_fusion.2 = (f32[2,4,512]{2,1,0:T(4,128)S(1)}, f32[2,1024,512,4]{2,1,3,0:T(8,128)}) fusion(pred[1024]{0:T(1024)(128)(4,1)S(1)} %fusion.116, bf16[1,512,2,4,128]{4,3,2,1,0:T(4,128)(2,1)S(1)} %constant_dynamic-slice_fusion.21, bf16[1024,2,128]{0,2,1:T(8,128)(2,1)S(1)} %squeeze.82), kind=kOutput, calls=%fused_computation.9.clone.1 | convolution fusion | flops 1086320640 | bytes 18367488 | tf_op jit(solution)/shard_map/while/body/eval_jaxpr/ikgd,jkd->kgij/dot_general | solution.py:144
  266.3 7.9 %fusion.120 = f32[2,128,4,512]{3,1,2,0:T(8,128)S(1)} fusion(f32[2,1024,512,4]{2,1,3,0:T(8,128)} %get-tuple-element.523, f32[2,4,512]{2,1,0:T(4,128)S(1)} %max.10, pred[1024]{0:T(1024)(128)(4,1)S(1)} %fusion.116, bf16[1024,2,128,1]{0,2,1,3:T(8,128)(2,1)S(1)} %reshape.367), kind=kOutput, calls=%fused_computation.16.clone.1 | convolution fusion | flops 1090519040 | bytes 19416064 | tf_op jit(solution)/shard_map/while/body/eval_jaxpr/kgij,jkd->ikgd/dot_general | solution.py:160
  274.2 8.1 %fusion.121 = f32[2,4,512]{2,1,0:T(4,128)S(1)} fusion(f32[2,1024,512,4]{2,1,3,0:T(8,128)} %get-tuple-element.523, f32[2,4,512]{2,1,0:T(4,128)S(1)} %max.10, pred[1024]{0:T(1024)(128)(4,1)S(1)} %fusion.116), kind=kLoop, calls=%fused_computation.12.clone.1 | loop fusion | flops 16773120 | bytes 16811008 | tf_op jit(solution)/shard_map/while/body/eval_jaxpr/reduce_sum | solution.py:159
  296.4 7.7 %bitcast_reduce_fusion.2 = (f32[2,4,512]{2,1,0:T(4,128)S(1)}, f32[2,1024,512,4]{2,1,3,0:T(8,128)}) fusion(pred[1024]{0:T(1024)(128)(4,1)S(1)} %fusion.116, bf16[1,512,2,4,128]{4,3,2,1,0:T(4,128)(2,1)S(1)} %constant_dynamic-slice_fusion.21, bf16[1024,2,128]{0,2,1:T(8,128)(2,1)S(1)} %squeeze.82), kind=kOutput, calls=%fused_computation.9.clone.1 | convolution fusion | flops 1086320640 | bytes 18367488 | tf_op jit(solution)/shard_map/while/body/eval_jaxpr/ikgd,jkd->kgij/dot_general | solution.py:144
  311.6 7.9 %fusion.120 = f32[2,128,4,512]{3,1,2,0:T(8,128)S(1)} fusion(f32[2,1024,512,4]{2,1,3,0:T(8,128)} %get-tuple-element.523, f32[2,4,512]{2,1,0:T(4,128)S(1)} %max.10, pred[1024]{0:T(1024)(128)(4,1)S(1)} %fusion.116, bf16[1024,2,128,1]{0,2,1,3:T(8,128)(2,1)S(1)} %reshape.367), kind=kOutput, calls=%fused_computation.16.clone.1 | convolution fusion | flops 1090519040 | bytes 19416064 | tf_op jit(solution)/shard_map/while/body/eval_jaxpr/kgij,jkd->ikgd/dot_general | solution.py:160
  319.5 8.1 %fusion.121 = f32[2,4,512]{2,1,0:T(4,128)S(1)} fusion(f32[2,1024,512,4]{2,1,3,0:T(8,128)} %get-tuple-element.523, f32[2,4,512]{2,1,0:T(4,128)S(1)} %max.10, pred[1024]{0:T(1024)(128)(4,1)S(1)} %fusion.116), kind=kLoop, calls=%fused_computation.12.clone.1 | loop fusion | flops 16773120 | bytes 16811008 | tf_op jit(solution)/shard_map/while/body/eval_jaxpr/reduce_sum | solution.py:159
  341.7 7.7 %bitcast_reduce_fusion.2 = (f32[2,4,512]{2,1,0:T(4,128)S(1)}, f32[2,1024,512,4]{2,1,3,0:T(8,128)}) fusion(pred[1024]{0:T(1024)(128)(4,1)S(1)} %fusion.116, bf16[1,512,2,4,128]{4,3,2,1,0:T(4,128)(2,1)S(1)} %constant_dynamic-slice_fusion.21, bf16[1024,2,128]{0,2,1:T(8,128)(2,1)S(1)} %squeeze.82), kind=kOutput, calls=%fused_computation.9.clone.1 | convolution fusion | flops 1086320640 | bytes 18367488 | tf_op jit(solution)/shard_map/while/body/eval_jaxpr/ikgd,jkd->kgij/dot_general | solution.py:144
  356.9 7.9 %fusion.120 = f32[2,128,4,512]{3,1,2,0:T(8,128)S(1)} fusion(f32[2,1024,512,4]{2,1,3,0:T(8,128)} %get-tuple-element.523, f32[2,4,512]{2,1,0:T(4,128)S(1)} %max.10, pred[1024]{0:T(1024)(128)(4,1)S(1)} %fusion.116, bf16[1024,2,128,1]{0,2,1,3:T(8,128)(2,1)S(1)} %reshape.367), kind=kOutput, calls=%fused_computation.16.clone.1 | convolution fusion | flops 1090519040 | bytes 19416064 | tf_op jit(solution)/shard_map/while/body/eval_jaxpr/kgij,jkd->ikgd/dot_general | solution.py:160
  364.8 8.1 %fusion.121 = f32[2,4,512]{2,1,0:T(4,128)S(1)} fusion(f32[2,1024,512,4]{2,1,3,0:T(8,128)} %get-tuple-element.523, f32[2,4,512]{2,1,0:T(4,128)S(1)} %max.10, pred[1024]{0:T(1024)(128)(4,1)S(1)} %fusion.116), kind=kLoop, calls=%fused_computation.12.clone.1 | loop fusion | flops 16773120 | bytes 16811008 | tf_op jit(solution)/shard_map/while/body/eval_jaxpr/reduce_sum | solution.py:159
  387.0 7.7 %bitcast_reduce_fusion.2 = (f32[2,4,512]{2,1,0:T(4,128)S(1)}, f32[2,1024,512,4]{2,1,3,0:T(8,128)}) fusion(pred[1024]{0:T(1024)(128)(4,1)S(1)} %fusion.116, bf16[1,512,2,4,128]{4,3,2,1,0:T(4,128)(2,1)S(1)} %constant_dynamic-slice_fusion.21, bf16[1024,2,128]{0,2,1:T(8,128)(2,1)S(1)} %squeeze.82), kind=kOutput, calls=%fused_computation.9.clone.1 | convolution fusion | flops 1086320640 | bytes 18367488 | tf_op jit(solution)/shard_map/while/body/eval_jaxpr/ikgd,jkd->kgij/dot_general | solution.py:144
  402.2 7.9 %fusion.120 = f32[2,128,4,512]{3,1,2,0:T(8,128)S(1)} fusion(f32[2,1024,512,4]{2,1,3,0:T(8,128)} %get-tuple-element.523, f32[2,4,512]{2,1,0:T(4,128)S(1)} %max.10, pred[1024]{0:T(1024)(128)(4,1)S(1)} %fusion.116, bf16[1024,2,128,1]{0,2,1,3:T(8,128)(2,1)S(1)} %reshape.367), kind=kOutput, calls=%fused_computation.16.clone.1 | convolution fusion | flops 1090519040 | bytes 19416064 | tf_op jit(solution)/shard_map/while/body/eval_jaxpr/kgij,jkd->ikgd/dot_general | solution.py:160
  410.1 8.1 %fusion.121 = f32[2,4,512]{2,1,0:T(4,128)S(1)} fusion(f32[2,1024,512,4]{2,1,3,0:T(8,128)} %get-tuple-element.523, f32[2,4,512]{2,1,0:T(4,128)S(1)} %max.10, pred[1024]{0:T(1024)(128)(4,1)S(1)} %fusion.116), kind=kLoop, calls=%fused_computation.12.clone.1 | loop fusion | flops 16773120 | bytes 16811008 | tf_op jit(solution)/shard_map/while/body/eval_jaxpr/reduce_sum | solution.py:159
  (480 shorter events, 262.0 us)
Async XLA Ops:
  0.6 25.1 %copy-start = (bf16[16,2,128,256]{3,2,1,0:T(8,128)(2,1)S(1)}, bf16[16,2,128,256]{3,2,1,0:T(8,128)(2,1)}, u32[]{:S(2)}) copy-start(bf16[16,2,128,256]{3,2,1,0:T(8,128)(2,1)} %param.24) | copy-start | bytes 6291460
  0.6 15.0 %copy-start.6 = (s32[16,8]{0,1:T(8,128)S(1)}, s32[16,8]{0,1:T(8,128)}, u32[]{:S(2)}) copy-start(s32[16,8]{0,1:T(8,128)} %param.34) | copy-start | bytes 1540
  0.7 15.1 %copy-start.7 = (s32[16,8,1]{0,2,1:T(1,128)S(1)}, s32[16,8,1]{0,2,1:T(1,128)}, u32[]{:S(2)}) copy-start(s32[16,8,1]{0,2,1:T(1,128)} %param.33) | copy-start | bytes 1540
  0.7 15.7 %copy-start.8 = (s32[16]{0:T(128)S(1)}, s32[16]{0:T(128)}, u32[]{:S(2)}) copy-start(s32[16]{0:T(128)} %param.35) | copy-start | bytes 196
  0.7 17.0 %copy-start.9 = (f32[16]{0:T(128)S(1)}, f32[16]{0:T(128)}, u32[]{:S(2)}) copy-start(f32[16]{0:T(128)} %param.30) | copy-start | bytes 196
  11.1 30.9 %all-to-all-start.1 = ((bf16[4,2,1024,128]{3,2,1,0:T(8,128)(2,1)}), bf16[4,2,1024,128]{3,2,1,0:T(8,128)(2,1)}, u32[]{:S(2)}, u32[]{:S(2)}) async-start(bf16[4,2,1024,128]{3,2,1,0:T(8,128)(2,1)} %select_select_fusion.1), calls=%async_computation.1 | async-start | bytes 4194304 | tf_op jit(solution)/shard_map/all_to_all | solution.py:115
  38.8 12.3 %copy-start.3 = (bf16[2048,2,128]{2,1,0:T(2,128)(2,1)S(1)}, bf16[2048,2,128]{2,1,0:T(2,128)(2,1)}, u32[]{:S(2)}) copy-start(bf16[2048,2,128]{2,1,0:T(2,128)(2,1)} %param.28) | copy-start | bytes 3145732
  38.8 12.3 %copy-start.4 = (f32[16]{0:T(128)S(1)}, f32[16]{0:T(128)}, u32[]{:S(2)}) copy-start(f32[16]{0:T(128)} %param.31) | copy-start | bytes 196
  42.0 190.3 %all-to-all-start = ((bf16[4,16,2,128,256]{4,3,2,1,0:T(8,128)(2,1)}), bf16[4,16,2,128,256]{4,3,2,1,0:T(8,128)(2,1)}, u32[]{:S(2)}, u32[]{:S(2)}) async-start(bf16[4,16,2,128,256]{4,3,2,1,0:T(8,128)(2,1)} %select_select_fusion), calls=%async_computation | async-start | bytes 16777216 | tf_op jit(solution)/shard_map/all_to_all | solution.py:103
  205.9 18.9 %copy-start.5 = (f32[1024]{0:T(1024)S(1)}, f32[1024]{0:T(1024)}, u32[]{:S(2)}) copy-start(f32[1024]{0:T(1024)} %param.32) | copy-start | bytes 12292
  274.1 8.2 %copy-start.2 = (f32[2,512,512,4]{2,1,3,0:T(8,128)S(1)}, f32[2,512,512,4]{2,1,3,0:T(8,128)}, u32[]{:S(2)}) copy-start(f32[2,512,512,4]{2,1,3,0:T(8,128)} %get-tuple-element.529) | copy-start | bytes 25165828 | tf_op jit(solution)/shard_map/while
  319.5 8.2 %copy-start.2 = (f32[2,512,512,4]{2,1,3,0:T(8,128)S(1)}, f32[2,512,512,4]{2,1,3,0:T(8,128)}, u32[]{:S(2)}) copy-start(f32[2,512,512,4]{2,1,3,0:T(8,128)} %get-tuple-element.529) | copy-start | bytes 25165828 | tf_op jit(solution)/shard_map/while
  364.8 8.2 %copy-start.2 = (f32[2,512,512,4]{2,1,3,0:T(8,128)S(1)}, f32[2,512,512,4]{2,1,3,0:T(8,128)}, u32[]{:S(2)}) copy-start(f32[2,512,512,4]{2,1,3,0:T(8,128)} %get-tuple-element.529) | copy-start | bytes 25165828 | tf_op jit(solution)/shard_map/while
  410.1 8.2 %copy-start.2 = (f32[2,512,512,4]{2,1,3,0:T(8,128)S(1)}, f32[2,512,512,4]{2,1,3,0:T(8,128)}, u32[]{:S(2)}) copy-start(f32[2,512,512,4]{2,1,3,0:T(8,128)} %get-tuple-element.529) | copy-start | bytes 25165828 | tf_op jit(solution)/shard_map/while
  424.3 1.6 copy-start.1
where the time goes:
time: 429 us; the launch traced here: 426 us
  matrix products  145 us (34%)
  local copies, waits for them, and re-layouts  123 us (29%)
  other arithmetic  110 us (26%)
  loops' own time  20.6 us (5%)
  blocking collectives  13 us (3%)
  starting transfers between devices  10.1 us (2%)
    reduce_sum x8, other arithmetic, attend(): total = jnp.sum(old_weights, axis=-1) + jnp.sum(new_weights, axis=-1)  39.3 us
    dot_general x16, matrix products, advance(): within = jnp.einsum('hij,jhp->ihp', mixing, block_in, precision=highest)  35.4 us
    dot_general x4, matrix products, attend(): jnp.einsum('kgij,jkd->ikgd', old_weights.astype(jnp.bfloat16), old_values...  31.5 us
    dot_general x4, matrix products, attend(): jnp.einsum('ikgd,jkd->kgij', query_rows, old_keys, preferred_element_type...  30.8 us
    dynamic_slice x48, local copies, waits for them, and re-layouts, stretch_scan(): lax.scan(advance, start_state, (input_blocks, in_blocks, out_blocks, step...  20.6 us
    dot_general x4, matrix products, attend(): jnp.einsum('ikgd,jkd->kgij', query_rows, new_keys, preferred_element_type...  19.6 us
    dynamic_update_slice x32, local copies, waits for them, and re-layouts, stretch_scan(): lax.scan(advance, start_state, (input_blocks, in_blocks, out_blocks, step...  16.7 us
    dynamic_update_slice x4, other arithmetic, body(): outputs, final_state = lax.map(mamba, request_ids)  14.9 us
  transfers between devices with their start and end apart: 2, of which 1 were waited for; matrix products, arithmetic and copies ran while one was open for 43% of the time, Pallas kernels for 0%

commit v1 on v0

v1 whole, which is shorter than its diff:
```python
import functools
import math

import jax
import jax.numpy as jnp
from jax import lax
from jax.experimental import pallas as pl
from jax.experimental.pallas import tpu as pltpu
from jax.sharding import PartitionSpec as P

HEAD_DIM = 128
SSM_DIM = 64
STRETCH = 128
REQUEST_NEW = 512
LOG2E = math.log2(math.e)

NT = (((1,), (1,)), ((), ()))


def scan_kernel(
    slot_ref, x_ref, gate_ref, in_ref, out_ref, step_ref, rate_ref, skip_ref, start_ref,
    mixed_ref, square_ref, final_ref, state,
):
    chunk = pl.program_id(1)
    pairs = x_ref.shape[1] // 128
    f32, bf16 = jnp.float32, jnp.bfloat16

    @pl.when(chunk == 0)
    def _():
        for p in range(pairs):
            cols = slice(p * 128, (p + 1) * 128)
            state[:, cols] = start_ref[0, cols, :].astype(f32).T

    row = lax.broadcasted_iota(jnp.int32, (128, 128), 0)
    lane = lax.broadcasted_iota(jnp.int32, (128, 128), 1)
    steps = step_ref[...]
    log_decay = steps * rate_ref[...]
    upper = (row <= lane).astype(f32)
    lower = (row >= lane).astype(f32)
    highest = lax.Precision.HIGHEST
    run_row = jnp.dot(log_decay, upper, precision=highest, preferred_element_type=f32)
    run_col = lax.dot_general(lower, log_decay, NT, precision=highest, preferred_element_type=f32)
    log_step = jnp.where(steps > 0, jnp.log(steps) * LOG2E, -1e30) - run_row
    weight = jnp.exp2(run_row[:, 127:128] + log_step)

    maps_in = in_ref[...]
    maps_out = out_ref[...]
    gram = lax.dot_general(maps_out, maps_in, NT, preferred_element_type=f32)
    gram = jnp.where(row >= lane, gram, 0.0)
    maps_in_t = maps_in.astype(f32).T
    low = lane < SSM_DIM
    squares = jnp.zeros((128, 128), f32)
    for p in range(pairs):
        cols = slice(p * 128, (p + 1) * 128)
        a, b = 2 * p, 2 * p + 1
        run_a = jnp.broadcast_to(run_col[:, a : a + 1], (128, 128))
        run_b = jnp.broadcast_to(run_col[:, b : b + 1], (128, 128))
        mix_a = (jnp.exp2(run_a + log_step[a : a + 1, :]) * gram).astype(bf16)
        mix_b = (jnp.exp2(run_b + log_step[b : b + 1, :]) * gram).astype(bf16)
        in_a = (maps_in_t * weight[a : a + 1, :]).astype(bf16)
        in_b = (maps_in_t * weight[b : b + 1, :]).astype(bf16)
        x = x_ref[:, cols].astype(f32)
        split = jnp.concatenate(
            [jnp.where(low, x, 0.0).astype(bf16), jnp.where(low, 0.0, x).astype(bf16)], axis=0
        )
        left = jnp.concatenate(
            [jnp.concatenate([mix_a, mix_b], axis=1), jnp.concatenate([in_a, in_b], axis=1)], axis=0
        )
        both = jnp.dot(left, split, preferred_element_type=f32)
        grown = jnp.exp2(jnp.where(low, run_a, run_b))
        old = state[:, cols]
        carried = jnp.dot(maps_out, old.astype(bf16), preferred_element_type=f32) * grown
        y = both[:128] + carried + skip_ref[:, cols] * x
        state[:, cols] = old * grown[127:128, :] + both[128:]
        gate = gate_ref[:, cols].astype(f32)
        mixed = y * gate / (1.0 + jnp.exp(-gate))
        squares = squares + mixed * mixed
        mixed_ref[:, cols] = mixed.astype(bf16)
    square_ref[0] = jnp.sum(squares.T, axis=0, keepdims=True)

    @pl.when(chunk == pl.num_programs(1) - 1)
    def _():
        for p in range(pairs):
            cols = slice(p * 128, (p + 1) * 128)
            final_ref[0, cols, :] = state[:, cols].T


def scan(slots, x, gate, maps_in, maps_out, steps, rates, skip, states):
    rows, channels = x.shape
    heads = steps.shape[0]
    requests = rows // REQUEST_NEW
    chunks = REQUEST_NEW // STRETCH
    wide = pl.BlockSpec((STRETCH, channels), lambda r, c, s: (r * chunks + c, 0))
    maps = pl.BlockSpec((STRETCH, 128), lambda r, c, s: (r * chunks + c, 0))
    return pl.pallas_call(
        scan_kernel,
        grid_spec=pltpu.PrefetchScalarGridSpec(
            num_scalar_prefetch=1,
            grid=(requests, chunks),
            in_specs=[
                wide,
                wide,
                maps,
                maps,
                pl.BlockSpec((heads, STRETCH), lambda r, c, s: (0, r * chunks + c)),
                pl.BlockSpec((heads, 1), lambda r, c, s: (0, 0)),
                pl.BlockSpec((1, channels), lambda r, c, s: (0, 0)),
                pl.BlockSpec((1, channels, 128), lambda r, c, s: (s[r], 0, 0)),
            ],
            out_specs=[
                wide,
                pl.BlockSpec((1, 1, STRETCH), lambda r, c, s: (r * chunks + c, 0, 0)),
                pl.BlockSpec((1, channels, 128), lambda r, c, s: (r, 0, 0)),
            ],
            scratch_shapes=[pltpu.VMEM((128, channels), jnp.float32)],
        ),
        out_shape=[
            jax.ShapeDtypeStruct((rows, channels), jnp.bfloat16),
            jax.ShapeDtypeStruct((rows // STRETCH, 1, STRETCH), jnp.float32),
            jax.ShapeDtypeStruct((requests, channels, 128), jnp.float32),
        ],
        compiler_params=pltpu.CompilerParams(vmem_limit_bytes=32 * 1024 * 1024),
        cost_estimate=pl.CostEstimate(
            flops=30_000_000_000, bytes_accessed=20_000_000, transcendentals=10_000_000
        ),
        name="scan",
    )(slots, x, gate, maps_in, maps_out, steps, rates, skip, states)


def attend_kernel(count, index_ref, length_ref, q_ref, new_k_ref, new_v_ref, *rest):
    blocks, out_ref, keys, values = rest[:count], rest[count], rest[count + 1], rest[count + 2]
    request = pl.program_id(0)
    matched = length_ref[request]
    f32, bf16 = jnp.float32, jnp.bfloat16
    tile = 128
    group = q_ref.shape[1] // HEAD_DIM
    prefix = count * tile
    scale = HEAD_DIM ** (-0.5) * LOG2E

    for j in range(count):
        rows = slice(j * tile, (j + 1) * tile)
        keys[rows, :] = blocks[j][0, 0]

        @pl.when(j < matched)
        def _():
            values[rows, :HEAD_DIM] = blocks[j][0, 1]
            values[rows, HEAD_DIM:] = jnp.ones((tile, HEAD_DIM), bf16)

        @pl.when(j >= matched)
        def _():
            values[rows, :] = jnp.zeros((tile, 2 * HEAD_DIM), bf16)

    keys[prefix:, :] = new_k_ref[...]
    values[prefix:, :HEAD_DIM] = new_v_ref[...]
    values[prefix:, HEAD_DIM:] = jnp.ones(new_v_ref.shape, bf16)

    place = lax.broadcasted_iota(jnp.int32, (group * tile, tile), 0) % tile
    causal = lax.broadcasted_iota(jnp.int32, (group * tile, tile), 1) <= place
    for t in range(q_ref.shape[0] // tile):
        rows = slice(t * tile, (t + 1) * tile)
        q = jnp.concatenate(
            [q_ref[rows, g * HEAD_DIM : (g + 1) * HEAD_DIM] for g in range(group)], axis=0
        )
        seen = prefix + t * tile
        old = lax.dot_general(q, keys[:seen, :], NT, preferred_element_type=f32)
        new = lax.dot_general(q, keys[seen : seen + tile, :], NT, preferred_element_type=f32)
        new = jnp.where(causal, new, -jnp.inf)
        peak = jnp.maximum(
            jnp.max(old, axis=1, keepdims=True), jnp.max(new, axis=1, keepdims=True)
        ) * scale
        weights = jnp.concatenate(
            [jnp.exp2(old * scale - peak).astype(bf16), jnp.exp2(new * scale - peak).astype(bf16)],
            axis=1,
        )
        total = jnp.dot(weights, values[: seen + tile, :], preferred_element_type=f32)
        result = (total[:, :HEAD_DIM] / total[:, HEAD_DIM:]).astype(bf16)
        for g in range(group):
            out_ref[rows, g * HEAD_DIM : (g + 1) * HEAD_DIM] = result[g * tile : (g + 1) * tile]


def attend(index, lengths, queries, new_k, new_v, blocks):
    rows, width = queries.shape
    requests = rows // REQUEST_NEW
    kv_heads = new_k.shape[1] // HEAD_DIM
    group_width = width // kv_heads
    block_rows = blocks.shape[2]
    count = index.shape[0] // requests
    wide = pl.BlockSpec((REQUEST_NEW, group_width), lambda r, h, i, n: (r, h))
    new = pl.BlockSpec((REQUEST_NEW, HEAD_DIM), lambda r, h, i, n: (r, h))

    def stored(j):
        return pl.BlockSpec(
            (1, 2, block_rows, HEAD_DIM), lambda r, h, i, n: (i[r * count + j], 0, 0, h)
        )

    key_rows = count * block_rows + REQUEST_NEW
    return pl.pallas_call(
        functools.partial(attend_kernel, count),
        grid_spec=pltpu.PrefetchScalarGridSpec(
            num_scalar_prefetch=2,
            grid=(requests, kv_heads),
            in_specs=[wide, new, new] + [stored(j) for j in range(count)],
            out_specs=wide,
            scratch_shapes=[
                pltpu.VMEM((key_rows, HEAD_DIM), jnp.bfloat16),
                pltpu.VMEM((key_rows, 2 * HEAD_DIM), jnp.bfloat16),
            ],
        ),
        out_shape=jax.ShapeDtypeStruct((rows, width), jnp.bfloat16),
        compiler_params=pltpu.CompilerParams(vmem_limit_bytes=48 * 1024 * 1024),
        cost_estimate=pl.CostEstimate(
            flops=60_000_000_000, bytes_accessed=20_000_000, transcendentals=25_000_000
        ),
        name="attend",
    )(index, lengths, queries, new_k, new_v, *([blocks] * count))


def body(
    queries,
    suffix_cache,
    cache_blocks,
    cache_states,
    ssm_input,
    gate_input,
    state_maps,
    step_size,
    decay_log,
    skip,
    norm_gain,
    hit_owner,
    hit_block,
    hit_len,
    saved_owner,
    saved_slot,
):
    position = lax.axis_index("store")
    requests = queries.shape[0] // REQUEST_NEW
    max_blocks = hit_block.shape[1]
    pool = cache_blocks.shape[0]
    saved = cache_states.shape[0]

    def mine(array):
        return lax.dynamic_slice_in_dim(array, position * requests, requests, 0)

    slots = mine(saved_owner[:, 0] * saved + saved_slot)
    lengths = mine(hit_len)
    index = mine(hit_owner[:, :, 0] * pool + hit_block)
    alive = jnp.arange(max_blocks)[None, :] < lengths[:, None]
    index = jnp.where(alive, index, index[:, :1]).reshape(-1)

    states = lax.all_gather(cache_states, "store", axis=0, tiled=True)
    blocks = lax.all_gather(cache_blocks, "store", axis=0, tiled=True)

    rates = (-jnp.exp(decay_log) * LOG2E)[:, None]
    skip_wide = jnp.repeat(skip, SSM_DIM)[None, :]
    mixed, squares, final_state = scan(
        slots, ssm_input, gate_input, state_maps[:, 0], state_maps[:, 1], step_size, rates,
        skip_wide, states,
    )
    squares = lax.psum(squares, "tensor").reshape(-1)
    attn_out = attend(index, lengths, queries, suffix_cache[:, 0], suffix_cache[:, 1], blocks)
    channels = ssm_input.shape[1] * lax.axis_size("tensor")
    ssm_out = (
        mixed.astype(jnp.float32) * lax.rsqrt(squares / channels + 1e-05)[:, None] * norm_gain
    ).astype(jnp.bfloat16)
    return (attn_out, ssm_out, final_state)


def solution(mesh):
    in_specs = (
        P(("groups", "store"), "tensor"),
        P(("groups", "store"), None, "tensor"),
        P(("groups", "store"), None, None, "tensor"),
        P(("groups", "store"), "tensor", None),
        P(("groups", "store"), "tensor"),
        P(("groups", "store"), "tensor"),
        P(("groups", "store"), None, None),
        P(("groups", "tensor"), "store"),
        P("tensor"),
        P("tensor"),
        P("tensor"),
        P("groups", None, None),
        P("groups", None),
        P("groups"),
        P("groups", None),
        P("groups"),
    )
    out_specs = (
        P(("groups", "store"), "tensor"),
        P(("groups", "store"), "tensor"),
        P(("groups", "store"), "tensor", None),
    )
    return jax.shard_map(body, mesh=mesh, in_specs=in_specs, out_specs=out_specs, check_vma=False)
```

time: 429 us -> 154 us (0.36)
  matrix products: 145 us -> 0 us
  local copies, waits for them, and re-layouts: 123 us -> 15.7 us
  other arithmetic: 110 us -> 6.38 us
  Pallas kernels: 0 us -> 61.3 us
  waiting for transfers between devices: 3.16 us -> 44 us
  loops' own time: 20.6 us -> 0 us
  between operations: 0.9 us -> 14.1 us
  starting transfers between devices: 10.1 us -> 0.08 us
    dot_general x80 -> x0, matrix products: 145 us -> none  [the longest x16 35.4 us: advance(): within = jnp.einsum('hij,jhp->ihp', mixing, block_in, precision=highest)]
    pallas_call x0 -> x2, Pallas kernels: none -> 61.3 us  [the longest x1 40 us: attend(): pl.pallas_call(functools.partial(attend_kernel, count), grid_spec=pltpu.P...]
    dynamic_slice x89 -> x3, local copies, waits for them, and re-layouts: 58.5 us -> 1.03 us  [mine(): return lax.dynamic_slice_in_dim(array, position * requests, requests, 0)]
    reduce_sum x13 -> x0, other arithmetic: 46 us -> none  [the longest x8 39.3 us: attend(): total = jnp.sum(old_weights, axis=-1) + jnp.sum(new_weights, axis=-1)]
    all_gather x0 -> x2, waiting for transfers between devices: none -> 42.7 us  [the longest x1 28.8 us: body(): states = lax.all_gather(cache_states, 'store', axis=0, tiled=True)]
    dynamic_update_slice x44 -> x0, local copies, waits for them, and re-layouts: 26.3 us -> none  [the longest x32 16.7 us: stretch_scan(): lax.scan(advance, start_state, (input_blocks, in_blocks, out_blocks, step...]
    another operation x6 -> x0, loops' own time: 20.6 us -> none  [the longest x1 10.6 us: body(): outputs, final_state = lax.map(mamba, request_ids)]
    gather x4 -> x0, local copies, waits for them, and re-layouts: 17.2 us -> none  [the longest x2 8.73 us: pack_slots(): taken = jnp.take(source, picked.reshape(-1), axis=0)]
  transfers between devices with their start and end apart: 2 -> 2, of which waited for: 1 -> 2; matrix products, arithmetic and copies ran while one was open for 43% -> 9% of each run, Pallas kernels for 0% -> 14%
where the time goes in v1:
time: 154 us
  Pallas kernels  61.3 us (40%)
  waiting for transfers between devices  44 us (29%)
  local copies, waits for them, and re-layouts  15.7 us (10%)
  between operations  14.1 us (9%)
  blocking collectives  11.8 us (8%)
  other arithmetic  6.38 us (4%)
    pallas_call x1, Pallas kernels, attend(): pl.pallas_call(functools.partial(attend_kernel, count), grid_spec=pltpu.P...  40 us
    all_gather x1, waiting for transfers between devices, body(): states = lax.all_gather(cache_states, 'store', axis=0, tiled=True)  28.8 us
    pallas_call x1, Pallas kernels, scan(): pl.pallas_call(scan_kernel, grid_spec=pltpu.PrefetchScalarGridSpec(num_sc...  21.4 us
    all_gather x1, waiting for transfers between devices, body(): blocks = lax.all_gather(cache_blocks, 'store', axis=0, tiled=True)  13.8 us
    psum x1, blocking collectives, body(): squares = lax.psum(squares, 'tensor').reshape(-1)  11.8 us
    unnamed x16, local copies, waits for them, and re-layouts  8.59 us
    convert_element_type x1, other arithmetic, body(): ssm_out = (mixed.astype(jnp.float32) * lax.rsqrt(squares / channels + 1e-...  4.25 us
  transfers between devices with their start and end apart: 2, of which 2 were waited for; matrix products, arithmetic and copies ran while one was open for 9% of the time, Pallas kernels for 14%

profile of v1, /device:TPU:0, one launch (start us, length us, event | category | flops | bytes accessed | tf_op | source)
XLA Modules:
  0.0 153.5 jit_solution(15541634986629163661)
XLA Ops:
  7.2 0.7 all-gather.5.cloned.1.call-update
  8.0 0.7 all-gather.3.cloned.1.call-update
  8.7 0.9 dynamic_slice.9.length_ref
  9.6 0.7 bitcast_add_fusion
  10.4 0.1 copy.27
  10.5 0.1 reshape.28.index_ref
  10.6 0.7 bitcast_add_fusion.1
  11.3 0.7 broadcast_in_dim.23
  12.1 0.7 multiply_bitcast_fusion
  12.8 0.1 copy.32.rate_ref
  12.9 1.5 fusion.2
  14.4 0.1 copy_bitcast_fusion.2
  14.5 3.0 %fusion.1 = (bf16[2048,1,256]{2,1,0:T(2,128)(2,1)S(1)}, bf16[2048,1,256]{2,1,0:T(2,128)(2,1)S(1)}) fusion(bf16[2048,2,256]{2,1,0:T(2,128)(2,1)S(1)} %copy-done.5), kind=kLoop, calls=%fused_computation.13 | loop fusion | bytes 4194304 | tf_op jit(solution)/shard_map/slice | solution.py:261
  17.5 0.5 copy_bitcast_fusion
  18.0 28.8 %all-gather.5.cloned.1.call-done.start_ref = bf16[16,1024,128]{2,1,0:T(8,128)(2,1)} async-done(((bf16[4,1024,128]{2,1,0:T(8,128)(2,1)}), bf16[16,1024,128]{2,1,0:T(8,128)(2,1)}) %all-gather.5.cloned.1.call-update) | async-done | bytes 4194320 | tf_op jit(solution)/shard_map/all_gather | solution.py:251
  46.8 2.2 %copy-done.1 = bf16[2048,1024]{1,0:T(8,128)(2,1)S(1)} copy-done((bf16[2048,1024]{1,0:T(8,128)(2,1)S(1)}, bf16[2048,1024]{1,0:T(8,128)(2,1)}, u32[]{:S(2)}) %copy-start.1) | copy-done | bytes 4194328
  49.0 2.2 %copy-done.2 = bf16[2048,1024]{1,0:T(8,128)(2,1)S(1)} copy-done((bf16[2048,1024]{1,0:T(8,128)(2,1)S(1)}, bf16[2048,1024]{1,0:T(8,128)(2,1)}, u32[]{:S(2)}) %copy-start.2) | copy-done | bytes 4194328
  51.2 2.2 %copy-done.3 = bf16[16,1024,128]{2,1,0:T(8,128)(2,1)S(1)} copy-done((bf16[16,1024,128]{2,1,0:T(8,128)(2,1)S(1)}, bf16[16,1024,128]{2,1,0:T(8,128)(2,1)}, u32[]{:S(2)}) %copy-start.3) | copy-done | bytes 4194328
  53.4 21.4 %scan.1 = (bf16[2048,1024]{1,0:T(8,128)(2,1)S(1)}, f32[16,1,128]{2,1,0:T(1,128)S(1)}, f32[4,1024,128]{2,1,0:T(8,128)}) custom-call(s32[4]{0:T(128)S(1)} %dynamic_slice.11.slot_ref, bf16[2048,1024]{1,0:T(8,128)(2,1)S(1)} %copy-done.1, bf16[2048,1024]{1,0:T(8,128)(2,1)S(1)} %copy-done.2, bf16[2048,128]{1,0:T(8,128)(2,1)S(1)} %get-tuple-element.16.in_ref, ...), custom_call_target="tpu_custom_call" | custom-call | flops 30000001024 | bytes 20000000 | tf_op jit(solution)/shard_map/scan/pallas_call | solution.py:95
  74.8 2.0 %copy-done = bf16[2048,1024]{1,0:T(8,128)(2,1)} copy-done((bf16[2048,1024]{1,0:T(8,128)(2,1)}, bf16[2048,1024]{1,0:T(8,128)(2,1)S(1)}, u32[]{:S(2)}) %copy-start) | copy-done | bytes 4194328
  76.8 11.8 %psum.7 = f32[16,1,128]{2,1,0:T(1,128)S(1)} all-reduce(f32[16,1,128]{2,1,0:T(1,128)S(1)} %get-tuple-element.7), channel_id=1, replica_groups=mesh['groups'=2,'store'=4,'tensor'=4] {'tensor'}, use_global_device_ids=true, to_apply=%region_0.1 | all-reduce | flops 2048 | bytes 16384 | tf_op jit(solution)/shard_map/psum | solution.py:260
  88.7 4.2 %multiply_convert_fusion = bf16[2048,1024]{1,0:T(8,128)(2,1)} fusion(bf16[2048,1024]{1,0:T(8,128)(2,1)} %copy-done, f32[1024]{0:T(1024)S(1)} %copy-done.7, f32[2048]{0:T(1024)S(1)} %bitcast.18), kind=kLoop, calls=%fused_computation | loop fusion | flops 8388608 | bytes 8400896 | tf_op jit(solution)/shard_map/convert_element_type | solution.py:265
  92.9 13.8 %all-gather.3.cloned.1.call-done.rest_0_.rest_1_.rest_2_.rest_3_.rest_4_.rest_5_.rest_6_.rest_7_ = bf16[64,2,128,256]{3,2,1,0:T(8,128)(2,1)} async-done(((bf16[16,2,128,256]{3,2,1,0:T(8,128)(2,1)}), bf16[64,2,128,256]{3,2,1,0:T(8,128)(2,1)}) %all-gather.3.cloned.1.call-update) | async-done | bytes 8388624 | tf_op jit(solution)/shard_map/all_gather | solution.py:252
  106.7 40.0 %attend.1 = bf16[2048,1024]{1,0:T(8,128)(2,1)} custom-call(s32[32]{0:T(128)S(1)} %reshape.28.index_ref, s32[4]{0:T(128)S(1)} %dynamic_slice.9.length_ref, bf16[2048,1024]{1,0:T(8,128)(2,1)} %q_ref.1, bf16[2048,256]{1,0:T(8,128)(2,1)S(1)} %get-tuple-element.14.new_k_ref, bf16[2048,256]{1,0:T(8,128)(2,1)S(1)} %get-tuple-element.13.new_v_ref, ...), custom_call_target="tpu_custom_call" | custom-call | flops 60000002048 | bytes 20000000 | tf_op jit(solution)/shard_map/attend/pallas_call | solution.py:197
  (20 shorter events, 0.4 us)
Async XLA Ops:
  7.2 5.7 %copy-start.6 = (bf16[2048,2,128]{2,1,0:T(2,128)(2,1)S(1)}, bf16[2048,2,128]{2,1,0:T(2,128)(2,1)}, u32[]{:S(2)}) copy-start(bf16[2048,2,128]{2,1,0:T(2,128)(2,1)} %param.22) | copy-start | bytes 3145732
  7.2 39.7 %all-gather.5.cloned.1.call-start = ((), (), s32[]{:S(2)}) async-start(), calls=%async_computation.1 | async-start | bytes 5242880 | tf_op jit(solution)/shard_map/all_gather | solution.py:251
  7.9 98.8 %all-gather.3.cloned.1.call-start = ((), (), s32[]{:S(2)}) async-start(), calls=%async_computation | async-start | bytes 10485760 | tf_op jit(solution)/shard_map/all_gather | solution.py:252
  8.7 5.9 %copy-start.5 = (bf16[2048,2,256]{2,1,0:T(2,128)(2,1)S(1)}, bf16[2048,2,256]{2,1,0:T(2,128)(2,1)}, u32[]{:S(2)}) copy-start(bf16[2048,2,256]{2,1,0:T(2,128)(2,1)} %param.17) | copy-start | bytes 6291460
  17.5 29.3 %copy-start.4 = (f32[16,2048]{1,0:T(8,128)S(1)}, f32[16,2048]{1,0:T(8,128)}, u32[]{:S(2)}) copy-start(f32[16,2048]{1,0:T(8,128)} %step_ref.1) | copy-start | bytes 393220
  46.8 2.2 %copy-start.1 = (bf16[2048,1024]{1,0:T(8,128)(2,1)S(1)}, bf16[2048,1024]{1,0:T(8,128)(2,1)}, u32[]{:S(2)}) copy-start(bf16[2048,1024]{1,0:T(8,128)(2,1)} %x_ref.1) | copy-start | bytes 12582916
  49.0 2.2 %copy-start.2 = (bf16[2048,1024]{1,0:T(8,128)(2,1)S(1)}, bf16[2048,1024]{1,0:T(8,128)(2,1)}, u32[]{:S(2)}) copy-start(bf16[2048,1024]{1,0:T(8,128)(2,1)} %gate_ref.1) | copy-start | bytes 12582916
  51.2 2.2 %copy-start.3 = (bf16[16,1024,128]{2,1,0:T(8,128)(2,1)S(1)}, bf16[16,1024,128]{2,1,0:T(8,128)(2,1)}, u32[]{:S(2)}) copy-start(bf16[16,1024,128]{2,1,0:T(8,128)(2,1)} %all-gather.5.cloned.1.call-done.start_ref) | copy-start | bytes 12582916
  53.4 35.2 %copy-start.7 = (f32[1024]{0:T(1024)S(1)}, f32[1024]{0:T(1024)}, u32[]{:S(2)}) copy-start(f32[1024]{0:T(1024)} %param.26) | copy-start | bytes 12292
  74.8 2.0 %copy-start = (bf16[2048,1024]{1,0:T(8,128)(2,1)}, bf16[2048,1024]{1,0:T(8,128)(2,1)S(1)}, u32[]{:S(2)}) copy-start(bf16[2048,1024]{1,0:T(8,128)(2,1)S(1)} %get-tuple-element.6) | copy-start | bytes 12582916
Sparse Core Ops, SparseCore 0:
  9.6 37.2 all-gather.4
  48.4 58.2 all-gather.2

commit v2 on v1

--- a/solution.py
+++ b/solution.py
@@ -18,18 +18,43 @@
 
 
 def scan_kernel(
-    slot_ref, x_ref, gate_ref, in_ref, out_ref, step_ref, rate_ref, skip_ref, start_ref,
-    mixed_ref, square_ref, final_ref, state,
+    stores, owner_ref, slot_ref, x_ref, gate_ref, in_ref, out_ref, step_ref, rate_ref, skip_ref,
+    *rest,
 ):
-    chunk = pl.program_id(1)
+    pools = rest[:stores]
+    mixed_ref, square_ref, final_ref, state, starts, sems = rest[stores:]
+    request, chunk = pl.program_id(0), pl.program_id(1)
+    requests = pl.num_programs(0)
+    position = lax.axis_index("store")
     pairs = x_ref.shape[1] // 128
     f32, bf16 = jnp.float32, jnp.bfloat16
 
+    def fetch(which):
+        place = position * requests + which
+        relative = owner_ref[place] ^ position
+        for k in range(stores):
+
+            @pl.when(relative == k)
+            def _():
+                pltpu.make_async_copy(
+                    pools[k].at[slot_ref[place]], starts.at[which % 2], sems.at[which % 2]
+                ).start()
+
+    @pl.when((chunk == 0) & (request == 0))
+    def _():
+        fetch(request)
+
     @pl.when(chunk == 0)
     def _():
+        now = request % 2
+        pltpu.make_async_copy(pools[0].at[0], starts.at[now], sems.at[now]).wait()
         for p in range(pairs):
             cols = slice(p * 128, (p + 1) * 128)
-            state[:, cols] = start_ref[0, cols, :].astype(f32).T
+            state[:, cols] = starts[now, cols, :].astype(f32).T
+
+        @pl.when(request + 1 < requests)
+        def _():
+            fetch(request + 1)
 
     row = lax.broadcasted_iota(jnp.int32, (128, 128), 0)
     lane = lax.broadcasted_iota(jnp.int32, (128, 128), 1)
@@ -85,65 +110,110 @@
             final_ref[0, cols, :] = state[:, cols].T
 
 
-def scan(slots, x, gate, maps_in, maps_out, steps, rates, skip, states):
+def scan(owners, slots, x, gate, maps_in, maps_out, steps, rates, skip, pools):
     rows, channels = x.shape
     heads = steps.shape[0]
     requests = rows // REQUEST_NEW
     chunks = REQUEST_NEW // STRETCH
-    wide = pl.BlockSpec((STRETCH, channels), lambda r, c, s: (r * chunks + c, 0))
-    maps = pl.BlockSpec((STRETCH, 128), lambda r, c, s: (r * chunks + c, 0))
+    wide = pl.BlockSpec((STRETCH, channels), lambda r, c, o, s: (r * chunks + c, 0))
+    maps = pl.BlockSpec((STRETCH, 128), lambda r, c, o, s: (r * chunks + c, 0))
     return pl.pallas_call(
-        scan_kernel,
+        functools.partial(scan_kernel, len(pools)),
         grid_spec=pltpu.PrefetchScalarGridSpec(
-            num_scalar_prefetch=1,
+            num_scalar_prefetch=2,
             grid=(requests, chunks),
             in_specs=[
                 wide,
                 wide,
                 maps,
                 maps,
-                pl.BlockSpec((heads, STRETCH), lambda r, c, s: (0, r * chunks + c)),
-                pl.BlockSpec((heads, 1), lambda r, c, s: (0, 0)),
-                pl.BlockSpec((1, channels), lambda r, c, s: (0, 0)),
-                pl.BlockSpec((1, channels, 128), lambda r, c, s: (s[r], 0, 0)),
-            ],
+                pl.BlockSpec((heads, STRETCH), lambda r, c, o, s: (0, r * chunks + c)),
+                pl.BlockSpec((heads, 1), lambda r, c, o, s: (0, 0)),
+                pl.BlockSpec((1, channels), lambda r, c, o, s: (0, 0)),
+            ]
+            + [pl.BlockSpec(memory_space=pl.ANY)] * len(pools),
             out_specs=[
                 wide,
-                pl.BlockSpec((1, 1, STRETCH), lambda r, c, s: (r * chunks + c, 0, 0)),
-                pl.BlockSpec((1, channels, 128), lambda r, c, s: (r, 0, 0)),
+                pl.BlockSpec((1, 1, STRETCH), lambda r, c, o, s: (r * chunks + c, 0, 0)),
+                pl.BlockSpec((1, channels, 128), lambda r, c, o, s: (r, 0, 0)),
             ],
-            scratch_shapes=[pltpu.VMEM((128, channels), jnp.float32)],
+            scratch_shapes=[
+                pltpu.VMEM((128, channels), jnp.float32),
+                pltpu.VMEM((2, channels, 128), jnp.bfloat16),
+                pltpu.SemaphoreType.DMA((2,)),
+            ],
         ),
         out_shape=[
             jax.ShapeDtypeStruct((rows, channels), jnp.bfloat16),
             jax.ShapeDtypeStruct((rows // STRETCH, 1, STRETCH), jnp.float32),
             jax.ShapeDtypeStruct((requests, channels, 128), jnp.float32),
         ],
-        compiler_params=pltpu.CompilerParams(vmem_limit_bytes=32 * 1024 * 1024),
+        compiler_params=pltpu.CompilerParams(vmem_limit_bytes=56 * 1024 * 1024),
         cost_estimate=pl.CostEstimate(
             flops=30_000_000_000, bytes_accessed=20_000_000, transcendentals=10_000_000
         ),
         name="scan",
-    )(slots, x, gate, maps_in, maps_out, steps, rates, skip, states)
-
-
-def attend_kernel(count, index_ref, length_ref, q_ref, new_k_ref, new_v_ref, *rest):
-    blocks, out_ref, keys, values = rest[:count], rest[count], rest[count + 1], rest[count + 2]
-    request = pl.program_id(0)
-    matched = length_ref[request]
+    )(owners, slots, x, gate, maps_in, maps_out, steps, rates, skip, *pools)
+
+
+def attend_kernel(
+    stores, count, owner_ref, block_ref, length_ref, q_ref, new_k_ref, new_v_ref, *rest
+):
+    pools = rest[:stores]
+    out_ref, key_slots, value_slots, sems = rest[stores:]
+    requests, kv_heads = pl.num_programs(0), pools[0].shape[3] // HEAD_DIM
+    request, head = pl.program_id(0), pl.program_id(1)
+    step = request * kv_heads + head
+    slot = step % 2
+    position = lax.axis_index("store")
+    matched = length_ref[position * requests + request]
+    keys, values = key_slots.at[slot], value_slots.at[slot]
     f32, bf16 = jnp.float32, jnp.bfloat16
     tile = 128
     group = q_ref.shape[1] // HEAD_DIM
     prefix = count * tile
     scale = HEAD_DIM ** (-0.5) * LOG2E
 
+    def fetch(which):
+        owner_row = position * requests + which // kv_heads
+        columns = pl.ds(pl.multiple_of((which % kv_heads) * HEAD_DIM, HEAD_DIM), HEAD_DIM)
+        into = which % 2
+        for j in range(count):
+            alive = j < length_ref[owner_row]
+            entry = owner_row * count + jnp.where(alive, j, 0)
+            relative, number = owner_ref[entry] ^ position, block_ref[entry]
+            rows = slice(j * tile, (j + 1) * tile)
+            for k in range(stores):
+
+                @pl.when(relative == k)
+                def _():
+                    pltpu.make_async_copy(
+                        pools[k].at[number, 0, :, columns],
+                        key_slots.at[into, rows, :],
+                        sems.at[into, j, 0],
+                    ).start()
+                    pltpu.make_async_copy(
+                        pools[k].at[number, 1, :, columns],
+                        value_slots.at[into, rows, :HEAD_DIM],
+                        sems.at[into, j, 1],
+                    ).start()
+
+    @pl.when(step == 0)
+    def _():
+        fetch(step)
+
+    @pl.when(step + 1 < requests * kv_heads)
+    def _():
+        fetch(step + 1)
+
     for j in range(count):
         rows = slice(j * tile, (j + 1) * tile)
-        keys[rows, :] = blocks[j][0, 0]
+        stored = pools[0].at[0, 0, :, :HEAD_DIM]
+        pltpu.make_async_copy(stored, keys.at[rows, :], sems.at[slot, j, 0]).wait()
+        pltpu.make_async_copy(stored, values.at[rows, :HEAD_DIM], sems.at[slot, j, 1]).wait()
 
         @pl.when(j < matched)
         def _():
-            values[rows, :HEAD_DIM] = blocks[j][0, 1]
             values[rows, HEAD_DIM:] = jnp.ones((tile, HEAD_DIM), bf16)
 
         @pl.when(j >= matched)
@@ -178,41 +248,55 @@
             out_ref[rows, g * HEAD_DIM : (g + 1) * HEAD_DIM] = result[g * tile : (g + 1) * tile]
 
 
-def attend(index, lengths, queries, new_k, new_v, blocks):
+def attend(owners, numbers, lengths, queries, new_k, new_v, pools):
     rows, width = queries.shape
     requests = rows // REQUEST_NEW
     kv_heads = new_k.shape[1] // HEAD_DIM
     group_width = width // kv_heads
-    block_rows = blocks.shape[2]
-    count = index.shape[0] // requests
-    wide = pl.BlockSpec((REQUEST_NEW, group_width), lambda r, h, i, n: (r, h))
-    new = pl.BlockSpec((REQUEST_NEW, HEAD_DIM), lambda r, h, i, n: (r, h))
-
-    def stored(j):
-        return pl.BlockSpec(
-            (1, 2, block_rows, HEAD_DIM), lambda r, h, i, n: (i[r * count + j], 0, 0, h)
-        )
-
-    key_rows = count * block_rows + REQUEST_NEW
+    count = owners.shape[0] // lengths.shape[0]
+    wide = pl.BlockSpec((REQUEST_NEW, group_width), lambda r, h, o, b, n: (r, h))
+    new = pl.BlockSpec((REQUEST_NEW, HEAD_DIM), lambda r, h, o, b, n: (r, h))
+    key_rows = count * pools[0].shape[2] + REQUEST_NEW
     return pl.pallas_call(
-        functools.partial(attend_kernel, count),
+        functools.partial(attend_kernel, len(pools), count),
         grid_spec=pltpu.PrefetchScalarGridSpec(
-            num_scalar_prefetch=2,
+            num_scalar_prefetch=3,
             grid=(requests, kv_heads),
-            in_specs=[wide, new, new] + [stored(j) for j in range(count)],
+            in_specs=[wide, new, new] + [pl.BlockSpec(memory_space=pl.ANY)] * len(pools),
             out_specs=wide,
             scratch_shapes=[
-                pltpu.VMEM((key_rows, HEAD_DIM), jnp.bfloat16),
-                pltpu.VMEM((key_rows, 2 * HEAD_DIM), jnp.bfloat16),
+                pltpu.VMEM((2, key_rows, HEAD_DIM), jnp.bfloat16),
+                pltpu.VMEM((2, key_rows, 2 * HEAD_DIM), jnp.bfloat16),
+                pltpu.SemaphoreType.DMA((2, count, 2)),
             ],
         ),
         out_shape=jax.ShapeDtypeStruct((rows, width), jnp.bfloat16),
-        compiler_params=pltpu.CompilerParams(vmem_limit_bytes=48 * 1024 * 1024),
+        compiler_params=pltpu.CompilerParams(vmem_limit_bytes=56 * 1024 * 1024),
         cost_estimate=pl.CostEstimate(
             flops=60_000_000_000, bytes_accessed=20_000_000, transcendentals=25_000_000
         ),
         name="attend",
-    )(index, lengths, queries, new_k, new_v, *([blocks] * count))
+    )(owners, numbers, lengths, queries, new_k, new_v, *pools)
+
+
+def swap(array, bit):
+    stores = lax.axis_size("store")
+    return lax.ppermute(array, "store", [(i, i ^ bit) for i in range(stores)])
+
+
+def from_own(array):
+    held, bit = {0: array}, 1
+    while bit < lax.axis_size("store"):
+        held[bit] = array
+        bit *= 2
+    return {k: swap(array, k) if k else array for k in sorted(held, reverse=True)}
+
+
+def relayed(held):
+    for k in range(1, lax.axis_size("store")):
+        if k not in held:
+            held[k] = swap(held[k & (k - 1)], k & -k)
+    return [held[k] for k in range(lax.axis_size("store"))]
 
 
 def body(
@@ -233,33 +317,30 @@
     saved_owner,
     saved_slot,
 ):
-    position = lax.axis_index("store")
-    requests = queries.shape[0] // REQUEST_NEW
-    max_blocks = hit_block.shape[1]
-    pool = cache_blocks.shape[0]
-    saved = cache_states.shape[0]
-
-    def mine(array):
-        return lax.dynamic_slice_in_dim(array, position * requests, requests, 0)
-
-    slots = mine(saved_owner[:, 0] * saved + saved_slot)
-    lengths = mine(hit_len)
-    index = mine(hit_owner[:, :, 0] * pool + hit_block)
-    alive = jnp.arange(max_blocks)[None, :] < lengths[:, None]
-    index = jnp.where(alive, index, index[:, :1]).reshape(-1)
-
-    states = lax.all_gather(cache_states, "store", axis=0, tiled=True)
-    blocks = lax.all_gather(cache_blocks, "store", axis=0, tiled=True)
+    first = from_own(cache_states)
+    cache_blocks, first = lax.optimization_barrier((cache_blocks, first))
+    states = relayed(first)
+    blocks = from_own(cache_blocks)
 
     rates = (-jnp.exp(decay_log) * LOG2E)[:, None]
     skip_wide = jnp.repeat(skip, SSM_DIM)[None, :]
     mixed, squares, final_state = scan(
-        slots, ssm_input, gate_input, state_maps[:, 0], state_maps[:, 1], step_size, rates,
+        saved_owner.reshape(-1), saved_slot, ssm_input, gate_input, state_maps[:, 0], state_maps[:, 1], step_size, rates,
         skip_wide, states,
     )
-    squares = lax.psum(squares, "tensor").reshape(-1)
-    attn_out = attend(index, lengths, queries, suffix_cache[:, 0], suffix_cache[:, 1], blocks)
-    channels = ssm_input.shape[1] * lax.axis_size("tensor")
+    blocks, squares = lax.optimization_barrier((blocks, squares))
+    blocks = relayed(blocks)
+    parts = lax.axis_size("tensor")
+    others = [
+        lax.ppermute(squares, "tensor", [(i, (i + k) % parts) for i in range(parts)])
+        for k in range(1, parts)
+    ]
+    attn_out = attend(
+        hit_owner.reshape(-1), hit_block.reshape(-1), hit_len, queries, suffix_cache[:, 0],
+        suffix_cache[:, 1], blocks,
+    )
+    squares = sum(others, squares).reshape(-1)
+    channels = ssm_input.shape[1] * parts
     ssm_out = (
         mixed.astype(jnp.float32) * lax.rsqrt(squares / channels + 1e-05)[:, None] * norm_gain
     ).astype(jnp.bfloat16)

time: 154 us -> 143 us (0.929)
  between operations: 14.1 us -> 0.75 us
  blocking collectives: 11.8 us -> 0 us
  starting transfers between devices: 0.08 us -> 10.1 us
  Pallas kernels: 61.3 us -> 65.6 us
  waiting for transfers between devices: 44 us -> 46.8 us
  other arithmetic: 6.38 us -> 4.84 us
    ppermute x0 -> x9, waiting for transfers between devices: none -> 46.8 us  [the longest x6 45.6 us: swap(): return lax.ppermute(array, 'store', [(i, i ^ bit) for i in range(stores)])]
    all_gather x2 -> x0, waiting for transfers between devices: 42.7 us -> none  [the longest x1 28.8 us: body(): states = lax.all_gather(cache_states, 'store', axis=0, tiled=True)]
    psum x1 -> x0, blocking collectives: 11.8 us -> none  [body(): squares = lax.psum(squares, 'tensor').reshape(-1)]
    ppermute x0 -> x9, starting transfers between devices: none -> 10.1 us  [the longest x6 5.16 us: swap(): return lax.ppermute(array, 'store', [(i, i ^ bit) for i in range(stores)])]
    unnamed x16 -> x20, local copies, waits for them, and re-layouts: 8.59 us -> 1.53 us
    pallas_call x2, Pallas kernels: 61.3 us -> 65.6 us  [the longest x1 40.9 us: attend(): pl.pallas_call(functools.partial(attend_kernel, len(pools), count), grid_...]
    slice x1, local copies, waits for them, and re-layouts: 1.48 us -> 3.46 us  [body(): state_maps[:, 1]]
  transfers between devices with their start and end apart: 2 -> 9, of which waited for: 2 -> 4; matrix products, arithmetic and copies ran while one was open for 9% -> 12% of each run, Pallas kernels for 14% -> 17%
where the time goes in v2:
time: 143 us; the launch traced here: 142 us
  Pallas kernels  65.6 us (46%)
  waiting for transfers between devices  46.8 us (33%)
  local copies, waits for them, and re-layouts  14.2 us (10%)
  starting transfers between devices  10.1 us (7%)
  other arithmetic  4.84 us (3%)
    ppermute x6, waiting for transfers between devices, swap(): return lax.ppermute(array, 'store', [(i, i ^ bit) for i in range(stores)])  45.6 us
    pallas_call x1, Pallas kernels, attend(): pl.pallas_call(functools.partial(attend_kernel, len(pools), count), grid_...  40.9 us
    pallas_call x1, Pallas kernels, scan(): pl.pallas_call(functools.partial(scan_kernel, len(pools)), grid_spec=pltp...  24.7 us
    ppermute x6, starting transfers between devices, swap(): return lax.ppermute(array, 'store', [(i, i ^ bit) for i in range(stores)])  5.16 us
    ppermute x3, starting transfers between devices, body(): lax.ppermute(squares, 'tensor', [(i, (i + k) % parts) for i in range(part...  4.89 us
    convert_element_type x1, other arithmetic, body(): ssm_out = (mixed.astype(jnp.float32) * lax.rsqrt(squares / channels + 1e-...  4.16 us
    slice x1, local copies, waits for them, and re-layouts, body(): state_maps[:, 1]  3.46 us
    slice x1, local copies, waits for them, and re-layouts, body(): suffix_cache[:, 1]  2.98 us
  transfers between devices with their start and end apart: 9, of which 4 were waited for; matrix products, arithmetic and copies ran while one was open for 12% of the time, Pallas kernels for 17%

profile of v2, /device:TPU:0, one launch (start us, length us, event | category | flops | bytes accessed | tf_op | source)
XLA Modules:
  0.0 142.2 jit_solution(6569936046258103245)
XLA Ops:
  0.6 0.5 collective-permute-start
  1.2 2.6 %collective-permute-start.1 = (bf16[4,1024,128]{2,1,0:T(8,128)(2,1)}, bf16[4,1024,128]{2,1,0:T(8,128)(2,1)}, u32[]{:S(2)}, u32[]{:S(2)}) collective-permute-start(bf16[4,1024,128]{2,1,0:T(8,128)(2,1)} %rest_0_), channel_id=1, source_target_pairs={{0,8},{4,12},{8,0},{12,4},{1,9},{5,13},{9,1},{13,5},{2,10},{6,14},... | collective-permute-start | bytes 3145736 | tf_op jit(solution)/shard_map/ppermute | solution.py:284
  3.8 24.1 %collective-permute-done.1.rest_2_ = bf16[4,1024,128]{2,1,0:T(8,128)(2,1)} collective-permute-done((bf16[4,1024,128]{2,1,0:T(8,128)(2,1)}, bf16[4,1024,128]{2,1,0:T(8,128)(2,1)}, u32[]{:S(2)}, u32[]{:S(2)}) %collective-permute-start.1) | collective-permute-done | bytes 1048608 | tf_op jit(solution)/shard_map/ppermute | solution.py:284
  27.8 0.7 multiply_bitcast_fusion
  28.5 0.7 copy.32.rate_ref
  29.2 0.7 broadcast_in_dim.9
  29.9 0.7 broadcast_in_dim_reshape.3.skip_ref
  30.6 3.5 %fusion.1 = (bf16[2048,1,128]{2,1,0:T(2,128)(2,1)S(1)}, bf16[2048,1,128]{2,1,0:T(2,128)(2,1)S(1)}) fusion(bf16[2048,2,128]{2,1,0:T(2,128)(2,1)} %param.22), kind=kLoop, calls=%fused_computation.8 | loop fusion | bytes 2097152 | tf_op jit(solution)/shard_map/slice | solution.py:328
  34.0 1.1 copy_bitcast_fusion.2
  35.2 1.8 %collective-permute-start.3 = (bf16[16,2,128,256]{3,2,1,0:T(8,128)(2,1)S(1)}, bf16[16,2,128,256]{3,2,1,0:T(8,128)(2,1)}, u32[]{:S(2)}, u32[]{:S(2)}) collective-permute-start(bf16[16,2,128,256]{3,2,1,0:T(8,128)(2,1)S(1)} %copy-done.5), channel_id=1, source_target_pairs={{0,8},{4,12},{8,0},{12,4},{1,9},{5,13},{9,1},{13,5},{2,10},{6,14},... | collective-permute-start | bytes 6291464 | tf_op jit(solution)/shard_map/ppermute | solution.py:284
  36.9 0.2 collective-permute-start.2
  37.2 24.7 %scan.1 = (bf16[2048,1024]{1,0:T(8,128)(2,1)}, f32[16,1,128]{2,1,0:T(1,128)}, f32[4,1024,128]{2,1,0:T(8,128)}) custom-call(s32[16]{0:T(128)} %bitcast.15, s32[16]{0:T(128)} %slot_ref.1, bf16[2048,1024]{1,0:T(8,128)(2,1)} %x_ref.1, bf16[2048,1024]{1,0:T(8,128)(2,1)} %gate_ref.1, bf16[2048,128]{1,0:T(8,128)(2,1)} %get-tuple-element.32.in_ref, ...), custom_call_target="tpu_custom_call" | custom-call | flops 30000001024 | bytes 20000000 | tf_op jit(solution)/shard_map/scan/pallas_call | solution.py:120
  61.8 21.5 %collective-permute-done.3.rest_2_ = bf16[16,2,128,256]{3,2,1,0:T(8,128)(2,1)} collective-permute-done((bf16[16,2,128,256]{3,2,1,0:T(8,128)(2,1)S(1)}, bf16[16,2,128,256]{3,2,1,0:T(8,128)(2,1)}, u32[]{:S(2)}, u32[]{:S(2)}) %collective-permute-start.3) | collective-permute-done | bytes 2097184 | tf_op jit(solution)/shard_map/ppermute | solution.py:284
  83.4 3.0 %fusion = (bf16[2048,1,256]{2,1,0:T(2,128)(2,1)S(1)}, bf16[2048,1,256]{2,1,0:T(2,128)(2,1)S(1)}) fusion(bf16[2048,2,256]{2,1,0:T(2,128)(2,1)S(1)} %copy-done), kind=kLoop, calls=%fused_computation.7 | loop fusion | bytes 4194304 | tf_op jit(solution)/shard_map/slice | solution.py:340
  86.5 3.9 %collective-permute-start.8 = (f32[16,1,128]{2,1,0:T(1,128)S(1)}, f32[16,1,128]{2,1,0:T(1,128)S(1)}, u32[]{:S(2)}, u32[]{:S(2)}) collective-permute-start(f32[16,1,128]{2,1,0:T(1,128)S(1)} %copy-done.1), channel_id=1, source_target_pairs={{0,3},{1,0},{2,1},{3,2},{4,7},{5,4},{6,5},{7,6},{8,11},{9,8},{10,9... | collective-permute-start | bytes 24584 | tf_op jit(solution)/shard_map/ppermute | solution.py:335
  90.3 1.0 collective-permute-start.6
  91.3 1.8 %copy_bitcast_fusion = (bf16[2048,256]{1,0:T(8,128)(2,1)}, bf16[2048,256]{1,0:T(8,128)(2,1)}) fusion(bf16[2048,1,256]{2,1,0:T(2,128)(2,1)S(1)} %get-tuple-element.25, bf16[2048,1,256]{2,1,0:T(2,128)(2,1)S(1)} %get-tuple-element.26), kind=kLoop, calls=%fused_computation.1 | loop fusion | bytes 4194304 | tf_op jit(solution)/shard_map/squeeze | solution.py:340
  93.2 0.6 reshape.29.owner_ref
  93.9 0.6 reshape.30.block_ref
  94.5 0.4 collective-permute-done.7
  94.9 0.9 collective-permute-done.6
  95.8 4.2 %multiply_convert_fusion = bf16[2048,1024]{1,0:T(8,128)(2,1)} fusion(bf16[2048,1024]{1,0:T(8,128)(2,1)} %get-tuple-element.22, f32[1024]{0:T(1024)S(1)} %copy-done.2, f32[2048]{0:T(1024)S(1)} %bitcast.14), kind=kLoop, calls=%fused_computation | loop fusion | flops 8388608 | bytes 8400896 | tf_op jit(solution)/shard_map/convert_element_type | solution.py:346
  100.0 1.3 copy-done.7
  101.3 40.9 %attend.1 = bf16[2048,1024]{1,0:T(8,128)(2,1)} custom-call(s32[128]{0:T(128)} %reshape.29.owner_ref, s32[128]{0:T(128)} %reshape.30.block_ref, s32[16]{0:T(128)} %length_ref.1, bf16[2048,1024]{1,0:T(8,128)(2,1)} %q_ref.1, bf16[2048,256]{1,0:T(8,128)(2,1)} %get-tuple-element.30.new_k_ref, bf16[2048,256]{1,0:T(8,128)(2,1)} %get-tuple-element.29.new_v_ref, ...), custom_call_target="tpu_custom_call" | custom-call | flops 60000002048 | bytes 20000000 | tf_op jit(solution)/shard_map/attend/pallas_call | solution.py:260
  (28 shorter events, 0.3 us)
Async XLA Ops:
  0.6 34.5 %copy-start.5 = (bf16[16,2,128,256]{3,2,1,0:T(8,128)(2,1)S(1)}, bf16[16,2,128,256]{3,2,1,0:T(8,128)(2,1)}, u32[]{:S(2)}) copy-start(bf16[16,2,128,256]{3,2,1,0:T(8,128)(2,1)} %rest_0_.1) | copy-start | bytes 6291460
  0.6 3.1 %collective-permute-start = (bf16[4,1024,128]{2,1,0:T(8,128)(2,1)}, bf16[4,1024,128]{2,1,0:T(8,128)(2,1)S(1)}, u32[]{:S(2)}, u32[]{:S(2)}) collective-permute-start(bf16[4,1024,128]{2,1,0:T(8,128)(2,1)} %rest_0_), channel_id=1, source_target_pairs={{0,4},{4,0},{8,12},{12,8},{1,5},{5,1},{9,13},{13,9},{2,6},{6,2},{1... | collective-permute-start | bytes 3145736 | tf_op jit(solution)/shard_map/ppermute | solution.py:284
  1.2 26.7 %collective-permute-start.1 = (bf16[4,1024,128]{2,1,0:T(8,128)(2,1)}, bf16[4,1024,128]{2,1,0:T(8,128)(2,1)}, u32[]{:S(2)}, u32[]{:S(2)}) collective-permute-start(bf16[4,1024,128]{2,1,0:T(8,128)(2,1)} %rest_0_), channel_id=1, source_target_pairs={{0,8},{4,12},{8,0},{12,4},{1,9},{5,13},{9,1},{13,5},{2,10},{6,14},... | collective-permute-start | bytes 3145736 | tf_op jit(solution)/shard_map/ppermute | solution.py:284
  3.8 33.4 %copy-start.8 = (bf16[4,1024,128]{2,1,0:T(8,128)(2,1)}, bf16[4,1024,128]{2,1,0:T(8,128)(2,1)S(1)}, u32[]{:S(2)}) copy-start(bf16[4,1024,128]{2,1,0:T(8,128)(2,1)S(1)} %collective-permute-done.rest_1_) | copy-start | bytes 3145732
  27.8 9.3 %collective-permute-start.4 = (bf16[4,1024,128]{2,1,0:T(8,128)(2,1)}, bf16[4,1024,128]{2,1,0:T(8,128)(2,1)}, u32[]{:S(2)}, u32[]{:S(2)}) collective-permute-start(bf16[4,1024,128]{2,1,0:T(8,128)(2,1)} %collective-permute-done.1.rest_2_), channel_id=1, source_target_pairs={{0,4},{4,0},{8,12},{12,8},{1,5},{5,1},{9,13},{13,9},{2,6},{6,2},{1... | collective-permute-start | bytes 3145736 | tf_op jit(solution)/shard_map/ppermute | solution.py:284
  35.2 48.2 %collective-permute-start.3 = (bf16[16,2,128,256]{3,2,1,0:T(8,128)(2,1)S(1)}, bf16[16,2,128,256]{3,2,1,0:T(8,128)(2,1)}, u32[]{:S(2)}, u32[]{:S(2)}) collective-permute-start(bf16[16,2,128,256]{3,2,1,0:T(8,128)(2,1)S(1)} %copy-done.5), channel_id=1, source_target_pairs={{0,8},{4,12},{8,0},{12,4},{1,9},{5,13},{9,1},{13,5},{2,10},{6,14},... | collective-permute-start | bytes 6291464 | tf_op jit(solution)/shard_map/ppermute | solution.py:284
  36.9 46.4 %collective-permute-start.2 = (bf16[16,2,128,256]{3,2,1,0:T(8,128)(2,1)S(1)}, bf16[16,2,128,256]{3,2,1,0:T(8,128)(2,1)S(1)}, u32[]{:S(2)}, u32[]{:S(2)}) collective-permute-start(bf16[16,2,128,256]{3,2,1,0:T(8,128)(2,1)S(1)} %copy-done.5), channel_id=1, source_target_pairs={{0,4},{4,0},{8,12},{12,8},{1,5},{5,1},{9,13},{13,9},{2,6},{6,2},{1... | collective-permute-start | bytes 6291464 | tf_op jit(solution)/shard_map/ppermute | solution.py:284
  37.2 46.3 %copy-start = (bf16[2048,2,256]{2,1,0:T(2,128)(2,1)S(1)}, bf16[2048,2,256]{2,1,0:T(2,128)(2,1)}, u32[]{:S(2)}) copy-start(bf16[2048,2,256]{2,1,0:T(2,128)(2,1)} %param.17) | copy-start | bytes 6291460
  83.3 3.1 %copy-start.6 = (bf16[16,2,128,256]{3,2,1,0:T(8,128)(2,1)}, bf16[16,2,128,256]{3,2,1,0:T(8,128)(2,1)S(1)}, u32[]{:S(2)}) copy-start(bf16[16,2,128,256]{3,2,1,0:T(8,128)(2,1)S(1)} %collective-permute-done.2.rest_1_) | copy-start | bytes 6291460
  83.3 3.1 %copy-start.1 = (f32[16,1,128]{2,1,0:T(1,128)S(1)}, f32[16,1,128]{2,1,0:T(1,128)}, u32[]{:S(2)}) copy-start(f32[16,1,128]{2,1,0:T(1,128)} %get-tuple-element.23) | copy-start | bytes 24580
  83.3 16.7 %collective-permute-start.5 = (bf16[16,2,128,256]{3,2,1,0:T(8,128)(2,1)}, bf16[16,2,128,256]{3,2,1,0:T(8,128)(2,1)S(1)}, u32[]{:S(2)}, u32[]{:S(2)}) collective-permute-start(bf16[16,2,128,256]{3,2,1,0:T(8,128)(2,1)} %collective-permute-done.3.rest_2_), channel_id=1, source_target_pairs={{0,4},{4,0},{8,12},{12,8},{1,5},{5,1},{9,13},{13,9},{2,6},{6,2},{1... | collective-permute-start | bytes 6291464 | tf_op jit(solution)/shard_map/ppermute | solution.py:284
  86.4 6.7 %copy-start.3 = (s32[16,8,1]{0,2,1:T(1,128)S(1)}, s32[16,8,1]{0,2,1:T(1,128)}, u32[]{:S(2)}) copy-start(s32[16,8,1]{0,2,1:T(1,128)} %param.27) | copy-start | bytes 1540
  86.4 7.4 %copy-start.4 = (s32[16,8]{0,1:T(8,128)S(1)}, s32[16,8]{0,1:T(8,128)}, u32[]{:S(2)}) copy-start(s32[16,8]{0,1:T(8,128)} %param.28) | copy-start | bytes 1540
  86.4 9.4 %copy-start.2 = (f32[1024]{0:T(1024)S(1)}, f32[1024]{0:T(1024)}, u32[]{:S(2)}) copy-start(f32[1024]{0:T(1024)} %param.26) | copy-start | bytes 12292
  86.5 8.1 %collective-permute-start.8 = (f32[16,1,128]{2,1,0:T(1,128)S(1)}, f32[16,1,128]{2,1,0:T(1,128)S(1)}, u32[]{:S(2)}, u32[]{:S(2)}) collective-permute-start(f32[16,1,128]{2,1,0:T(1,128)S(1)} %copy-done.1), channel_id=1, source_target_pairs={{0,3},{1,0},{2,1},{3,2},{4,7},{5,4},{6,5},{7,6},{8,11},{9,8},{10,9... | collective-permute-start | bytes 24584 | tf_op jit(solution)/shard_map/ppermute | solution.py:335
  90.3 4.5 %collective-permute-start.7 = (f32[16,1,128]{2,1,0:T(1,128)S(1)}, f32[16,1,128]{2,1,0:T(1,128)S(1)}, u32[]{:S(2)}, u32[]{:S(2)}) collective-permute-start(f32[16,1,128]{2,1,0:T(1,128)S(1)} %copy-done.1), channel_id=1, source_target_pairs={{0,2},{1,3},{2,0},{3,1},{4,6},{5,7},{6,4},{7,5},{8,10},{9,11},{10,... | collective-permute-start | bytes 24584 | tf_op jit(solution)/shard_map/ppermute | solution.py:335
  90.3 5.4 %collective-permute-start.6 = (f32[16,1,128]{2,1,0:T(1,128)S(1)}, f32[16,1,128]{2,1,0:T(1,128)S(1)}, u32[]{:S(2)}, u32[]{:S(2)}) collective-permute-start(f32[16,1,128]{2,1,0:T(1,128)S(1)} %copy-done.1), channel_id=1, source_target_pairs={{0,1},{1,2},{2,3},{3,0},{4,5},{5,6},{6,7},{7,4},{8,9},{9,10},{10,1... | collective-permute-start | bytes 24584 | tf_op jit(solution)/shard_map/ppermute | solution.py:335
  100.0 1.3 copy-start.7

commit v3 on v2

--- a/solution.py
+++ b/solution.py
@@ -160,11 +160,9 @@
     stores, count, owner_ref, block_ref, length_ref, q_ref, new_k_ref, new_v_ref, *rest
 ):
     pools = rest[:stores]
-    out_ref, key_slots, value_slots, sems = rest[stores:]
-    requests, kv_heads = pl.num_programs(0), pools[0].shape[3] // HEAD_DIM
-    request, head = pl.program_id(0), pl.program_id(1)
-    step = request * kv_heads + head
-    slot = step % 2
+    out_ref, key_slots, value_slots, sems = rest[-4:]
+    requests, request = pl.num_programs(0), pl.program_id(0)
+    slot = request % 2
     position = lax.axis_index("store")
     matched = length_ref[position * requests + request]
     keys, values = key_slots.at[slot], value_slots.at[slot]
@@ -175,8 +173,7 @@
     scale = HEAD_DIM ** (-0.5) * LOG2E
 
     def fetch(which):
-        owner_row = position * requests + which // kv_heads
-        columns = pl.ds(pl.multiple_of((which % kv_heads) * HEAD_DIM, HEAD_DIM), HEAD_DIM)
+        owner_row = position * requests + which
         into = which % 2
         for j in range(count):
             alive = j < length_ref[owner_row]
@@ -188,27 +185,27 @@
                 @pl.when(relative == k)
                 def _():
                     pltpu.make_async_copy(
-                        pools[k].at[number, 0, :, columns],
+                        pools[k].at[number, 0],
                         key_slots.at[into, rows, :],
                         sems.at[into, j, 0],
                     ).start()
                     pltpu.make_async_copy(
-                        pools[k].at[number, 1, :, columns],
+                        pools[k].at[number, 1],
                         value_slots.at[into, rows, :HEAD_DIM],
                         sems.at[into, j, 1],
                     ).start()
 
-    @pl.when(step == 0)
-    def _():
-        fetch(step)
-
-    @pl.when(step + 1 < requests * kv_heads)
-    def _():
-        fetch(step + 1)
+    @pl.when(request == 0)
+    def _():
+        fetch(request)
+
+    @pl.when(request + 1 < requests)
+    def _():
+        fetch(request + 1)
 
     for j in range(count):
         rows = slice(j * tile, (j + 1) * tile)
-        stored = pools[0].at[0, 0, :, :HEAD_DIM]
+        stored = pools[0].at[0, 0]
         pltpu.make_async_copy(stored, keys.at[rows, :], sems.at[slot, j, 0]).wait()
         pltpu.make_async_copy(stored, values.at[rows, :HEAD_DIM], sems.at[slot, j, 1]).wait()
 
@@ -248,21 +245,21 @@
             out_ref[rows, g * HEAD_DIM : (g + 1) * HEAD_DIM] = result[g * tile : (g + 1) * tile]
 
 
-def attend(owners, numbers, lengths, queries, new_k, new_v, pools):
+def attend(head, done, owners, numbers, lengths, queries, new_k, new_v, pools):
     rows, width = queries.shape
     requests = rows // REQUEST_NEW
     kv_heads = new_k.shape[1] // HEAD_DIM
     group_width = width // kv_heads
     count = owners.shape[0] // lengths.shape[0]
-    wide = pl.BlockSpec((REQUEST_NEW, group_width), lambda r, h, o, b, n: (r, h))
-    new = pl.BlockSpec((REQUEST_NEW, HEAD_DIM), lambda r, h, o, b, n: (r, h))
+    wide = pl.BlockSpec((REQUEST_NEW, group_width), lambda r, o, b, n: (r, head))
+    new = pl.BlockSpec((REQUEST_NEW, HEAD_DIM), lambda r, o, b, n: (r, head))
     key_rows = count * pools[0].shape[2] + REQUEST_NEW
     return pl.pallas_call(
         functools.partial(attend_kernel, len(pools), count),
         grid_spec=pltpu.PrefetchScalarGridSpec(
             num_scalar_prefetch=3,
-            grid=(requests, kv_heads),
-            in_specs=[wide, new, new] + [pl.BlockSpec(memory_space=pl.ANY)] * len(pools),
+            grid=(requests,),
+            in_specs=[wide, new, new] + [pl.BlockSpec(memory_space=pl.ANY)] * (len(pools) + len(done)),
             out_specs=wide,
             scratch_shapes=[
                 pltpu.VMEM((2, key_rows, HEAD_DIM), jnp.bfloat16),
@@ -273,10 +270,11 @@
         out_shape=jax.ShapeDtypeStruct((rows, width), jnp.bfloat16),
         compiler_params=pltpu.CompilerParams(vmem_limit_bytes=56 * 1024 * 1024),
         cost_estimate=pl.CostEstimate(
-            flops=60_000_000_000, bytes_accessed=20_000_000, transcendentals=25_000_000
+            flops=30_000_000_000, bytes_accessed=20_000_000, transcendentals=12_000_000
         ),
+        input_output_aliases={6 + len(pools): 0} if done else {},
         name="attend",
-    )(owners, numbers, lengths, queries, new_k, new_v, *pools)
+    )(owners, numbers, lengths, queries, new_k, new_v, *pools, *done)
 
 
 def swap(array, bit):
@@ -317,28 +315,41 @@
     saved_owner,
     saved_slot,
 ):
+    kv_heads = cache_blocks.shape[3] // HEAD_DIM
     first = from_own(cache_states)
-    cache_blocks, first = lax.optimization_barrier((cache_blocks, first))
-    states = relayed(first)
-    blocks = from_own(cache_blocks)
-
+    pieces = [cache_blocks[..., h * HEAD_DIM : (h + 1) * HEAD_DIM] for h in range(kv_heads)]
+    new_k, new_v = suffix_cache[:, 0], suffix_cache[:, 1]
+    maps_in, maps_out = state_maps[:, 0], state_maps[:, 1]
     rates = (-jnp.exp(decay_log) * LOG2E)[:, None]
     skip_wide = jnp.repeat(skip, SSM_DIM)[None, :]
+    hits = hit_owner.reshape(-1), hit_block.reshape(-1)
+    first, pieces, new_k, new_v, maps_in, maps_out, rates, skip_wide, hits = (
+        lax.optimization_barrier(
+            (first, pieces, new_k, new_v, maps_in, maps_out, rates, skip_wide, hits)
+        )
+    )
+    states = relayed(first)
+    blocks = from_own(pieces[0])
+
     mixed, squares, final_state = scan(
-        saved_owner.reshape(-1), saved_slot, ssm_input, gate_input, state_maps[:, 0], state_maps[:, 1], step_size, rates,
-        skip_wide, states,
+        saved_owner.reshape(-1), saved_slot, ssm_input, gate_input, maps_in, maps_out, step_size,
+        rates, skip_wide, states,
     )
-    blocks, squares = lax.optimization_barrier((blocks, squares))
-    blocks = relayed(blocks)
+    blocks, squares, pieces = lax.optimization_barrier((blocks, squares, pieces))
     parts = lax.axis_size("tensor")
     others = [
         lax.ppermute(squares, "tensor", [(i, (i + k) % parts) for i in range(parts)])
         for k in range(1, parts)
     ]
-    attn_out = attend(
-        hit_owner.reshape(-1), hit_block.reshape(-1), hit_len, queries, suffix_cache[:, 0],
-        suffix_cache[:, 1], blocks,
-    )
+    done = []
+    for h in range(kv_heads):
+        later = from_own(pieces[h + 1]) if h + 1 < kv_heads else None
+        done = [
+            attend(h, done, *hits, hit_len, queries, new_k, new_v, relayed(blocks))
+        ]
+        if later is not None:
+            blocks, done = lax.optimization_barrier((later, done))
+    attn_out = done[0]
     squares = sum(others, squares).reshape(-1)
     channels = ssm_input.shape[1] * parts
     ssm_out = (

time: 143 us -> 118 us (0.83)
  waiting for transfers between devices: 46.8 us -> 16.1 us
  Pallas kernels: 65.6 us -> 68.9 us
  starting transfers between devices: 10.1 us -> 12.1 us
  local copies, waits for them, and re-layouts: 14.2 us -> 16.1 us
  other arithmetic: 4.84 us -> 3.26 us
    ppermute x6 -> x9, waiting for transfers between devices: 45.6 us -> 11.6 us  [swap(): return lax.ppermute(array, 'store', [(i, i ^ bit) for i in range(stores)])]
    pallas_call x1 -> x2, Pallas kernels: 40.9 us -> 44.4 us  [attend(): pl.pallas_call(functools.partial(attend_kernel, len(pools), count), grid_...]
    ppermute x3, waiting for transfers between devices: 1.28 us -> 4.43 us  [body(): lax.ppermute(squares, 'tensor', [(i, (i + k) % parts) for i in range(part...]
    unnamed x20 -> x24, local copies, waits for them, and re-layouts: 1.53 us -> 3.52 us
    ppermute x6 -> x9, starting transfers between devices: 5.16 us -> 7.15 us  [swap(): return lax.ppermute(array, 'store', [(i, i ^ bit) for i in range(stores)])]
    convert_element_type x1, other arithmetic: 4.16 us -> 2.58 us  [body(): ssm_out = (mixed.astype(jnp.float32) * lax.rsqrt(squares / channels + 1e-...]
    slice x2 -> x3, local copies, waits for them, and re-layouts: 6.44 us -> 6.31 us  [the longest x1 2.98 us: body(): new_k, new_v = (suffix_cache[:, 0], suffix_cache[:, 1])]
  transfers between devices with their start and end apart: 9 -> 12, of which waited for: 4 -> 7; matrix products, arithmetic and copies ran while one was open for 12% -> 15% of each run, Pallas kernels for 17% -> 40%
where the time goes in v3:
time: 118 us; the launch traced here: 117 us
  Pallas kernels  68.9 us (58%)
  local copies, waits for them, and re-layouts  16.1 us (14%)
  waiting for transfers between devices  16.1 us (14%)
  starting transfers between devices  12.1 us (10%)
  other arithmetic  3.26 us (3%)
    pallas_call x2, Pallas kernels, attend(): pl.pallas_call(functools.partial(attend_kernel, len(pools), count), grid_...  44.4 us
    pallas_call x1, Pallas kernels, scan(): pl.pallas_call(functools.partial(scan_kernel, len(pools)), grid_spec=pltp...  24.5 us
    ppermute x9, waiting for transfers between devices, swap(): return lax.ppermute(array, 'store', [(i, i ^ bit) for i in range(stores)])  11.6 us
    ppermute x9, starting transfers between devices, swap(): return lax.ppermute(array, 'store', [(i, i ^ bit) for i in range(stores)])  7.15 us
    ppermute x3, starting transfers between devices, body(): lax.ppermute(squares, 'tensor', [(i, (i + k) % parts) for i in range(part...  4.9 us
    ppermute x3, waiting for transfers between devices, body(): lax.ppermute(squares, 'tensor', [(i, (i + k) % parts) for i in range(part...  4.43 us
    unnamed x24, local copies, waits for them, and re-layouts  3.52 us
    slice x1, local copies, waits for them, and re-layouts, body(): new_k, new_v = (suffix_cache[:, 0], suffix_cache[:, 1])  2.98 us
  transfers between devices with their start and end apart: 12, of which 7 were waited for; matrix products, arithmetic and copies ran while one was open for 15% of the time, Pallas kernels for 40%

profile of v3, /device:TPU:0, one launch (start us, length us, event | category | flops | bytes accessed | tf_op | source)
XLA Modules:
  0.0 117.4 jit_solution(2724543973986461801)
XLA Ops:
  1.2 2.6 %collective-permute-start.1 = (bf16[4,1024,128]{2,1,0:T(8,128)(2,1)}, bf16[4,1024,128]{2,1,0:T(8,128)(2,1)}, u32[]{:S(2)}, u32[]{:S(2)}) collective-permute-start(bf16[4,1024,128]{2,1,0:T(8,128)(2,1)} %rest_0_), channel_id=1, source_target_pairs={{0,8},{4,12},{8,0},{12,4},{1,9},{5,13},{9,1},{13,5},{2,10},{6,14},... | collective-permute-start | bytes 3145736 | tf_op jit(solution)/shard_map/ppermute | solution.py:282
  4.4 0.7 broadcast_in_dim.9
  5.8 0.8 copy.31
  7.2 0.8 copy.32
  8.0 0.7 reshape.30.block_ref
  8.7 1.8 %fusion.1 = (bf16[16,2,128,128]{3,2,1,0:T(8,128)(2,1)S(1)}, bf16[16,2,128,128]{3,2,1,0:T(8,128)(2,1)S(1)}) fusion(bf16[16,2,128,256]{3,2,1,0:T(8,128)(2,1)} %param.18), kind=kLoop, calls=%fused_computation.8 | loop fusion | bytes 4194304 | tf_op jit(solution)/shard_map/slice | solution.py:320
  10.5 1.5 %fusion.2 = (bf16[2048,1,128]{2,1,0:T(2,128)(2,1)S(1)}, bf16[2048,1,128]{2,1,0:T(2,128)(2,1)S(1)}) fusion(bf16[2048,2,128]{2,1,0:T(2,128)(2,1)S(1)} %copy-done.2), kind=kLoop, calls=%fused_computation.9 | loop fusion | bytes 2097152 | tf_op jit(solution)/shard_map/slice | solution.py:322
  12.0 3.0 %fusion = (bf16[2048,1,256]{2,1,0:T(2,128)(2,1)S(1)}, bf16[2048,1,256]{2,1,0:T(2,128)(2,1)S(1)}) fusion(bf16[2048,2,256]{2,1,0:T(2,128)(2,1)S(1)} %copy-done), kind=kLoop, calls=%fused_computation.7 | loop fusion | bytes 4194304 | tf_op jit(solution)/shard_map/slice | solution.py:321
  15.0 1.2 %copy_bitcast_fusion.2 = (bf16[2048,128]{1,0:T(8,128)(2,1)}, bf16[2048,128]{1,0:T(8,128)(2,1)}) fusion(bf16[2048,1,128]{2,1,0:T(2,128)(2,1)S(1)} %get-tuple-element.57, bf16[2048,1,128]{2,1,0:T(2,128)(2,1)S(1)} %get-tuple-element.58), kind=kLoop, calls=%fused_computation.3 | loop fusion | bytes 2097152 | tf_op jit(solution)/shard_map/squeeze | solution.py:322
  16.2 1.7 %copy_bitcast_fusion = (bf16[2048,256]{1,0:T(8,128)(2,1)}, bf16[2048,256]{1,0:T(8,128)(2,1)}) fusion(bf16[2048,1,256]{2,1,0:T(2,128)(2,1)S(1)} %get-tuple-element.53, bf16[2048,1,256]{2,1,0:T(2,128)(2,1)S(1)} %get-tuple-element.54), kind=kLoop, calls=%fused_computation.1 | loop fusion | bytes 4194304 | tf_op jit(solution)/shard_map/squeeze | solution.py:321
  17.9 9.9 %collective-permute-done.1.rest_2_ = bf16[4,1024,128]{2,1,0:T(8,128)(2,1)} collective-permute-done((bf16[4,1024,128]{2,1,0:T(8,128)(2,1)}, bf16[4,1024,128]{2,1,0:T(8,128)(2,1)}, u32[]{:S(2)}, u32[]{:S(2)}) %collective-permute-start.1) | collective-permute-done | bytes 1048608 | tf_op jit(solution)/shard_map/ppermute | solution.py:282
  27.8 1.8 %collective-permute-start.3 = (bf16[16,2,128,128]{3,2,1,0:T(8,128)(2,1)S(1)}, bf16[16,2,128,128]{3,2,1,0:T(8,128)(2,1)}, u32[]{:S(2)}, u32[]{:S(2)}) collective-permute-start(bf16[16,2,128,128]{3,2,1,0:T(8,128)(2,1)S(1)} %get-tuple-element.43.rest_0_), channel_id=1, source_target_pairs={{0,8},{4,12},{8,0},{12,4},{1,9},{5,13},{9,1},{13,5},{2,10},{6,14},... | collective-permute-start | bytes 3145736 | tf_op jit(solution)/shard_map/ppermute | solution.py:282
  30.8 24.5 %scan.1 = (bf16[2048,1024]{1,0:T(8,128)(2,1)}, f32[16,1,128]{2,1,0:T(1,128)}, f32[4,1024,128]{2,1,0:T(8,128)}) custom-call(s32[16]{0:T(128)} %bitcast.15, s32[16]{0:T(128)} %slot_ref.1, bf16[2048,1024]{1,0:T(8,128)(2,1)} %x_ref.1, bf16[2048,1024]{1,0:T(8,128)(2,1)} %gate_ref.1, bf16[2048,128]{1,0:T(8,128)(2,1)} %get-tuple-element.33.in_ref, ...), custom_call_target="tpu_custom_call" | custom-call | flops 30000001024 | bytes 20000000 | tf_op jit(solution)/shard_map/scan/pallas_call | solution.py:120
  55.4 1.0 copy-done.10
  56.5 1.8 %collective-permute-start.6 = (bf16[16,2,128,128]{3,2,1,0:T(8,128)(2,1)S(1)}, bf16[16,2,128,128]{3,2,1,0:T(8,128)(2,1)S(1)}, u32[]{:S(2)}, u32[]{:S(2)}) collective-permute-start(bf16[16,2,128,128]{3,2,1,0:T(8,128)(2,1)S(1)} %get-tuple-element.46.rest_0_), channel_id=1, source_target_pairs={{0,8},{4,12},{8,0},{12,4},{1,9},{5,13},{9,1},{13,5},{2,10},{6,14},... | collective-permute-start | bytes 3145736 | tf_op jit(solution)/shard_map/ppermute | solution.py:282
  58.4 1.0 collective-permute-done.7.rest_3_
  59.4 22.2 %attend.2.rest_4_ = bf16[2048,1024]{1,0:T(8,128)(2,1)} custom-call(s32[128]{0:T(128)} %reshape.29.owner_ref, s32[128]{0:T(128)} %reshape.30.block_ref, s32[16]{0:T(128)} %length_ref.3, bf16[2048,1024]{1,0:T(8,128)(2,1)} %q_ref.3, bf16[2048,256]{1,0:T(8,128)(2,1)} %get-tuple-element.30.new_k_ref, bf16[2048,256]{1,0:T(8,128)(2,1)} %get-tuple-element.31.new_v_ref, ...), custom_call_target="tpu_custom_call" | custom-call | flops 30000001024 | bytes 20000000 | tf_op jit(solution)/shard_map/attend/pallas_call | solution.py:257
  82.1 3.9 %collective-permute-start.11 = (f32[16,1,128]{2,1,0:T(1,128)S(1)}, f32[16,1,128]{2,1,0:T(1,128)S(1)}, u32[]{:S(2)}, u32[]{:S(2)}) collective-permute-start(f32[16,1,128]{2,1,0:T(1,128)S(1)} %copy-done.5), channel_id=1, source_target_pairs={{0,3},{1,0},{2,1},{3,2},{4,7},{5,4},{6,5},{7,6},{8,11},{9,8},{10,9... | collective-permute-start | bytes 24584 | tf_op jit(solution)/shard_map/ppermute | solution.py:341
  86.0 1.0 collective-permute-start.9
  87.3 3.2 %collective-permute-done.10 = f32[16,1,128]{2,1,0:T(1,128)S(1)} collective-permute-done((f32[16,1,128]{2,1,0:T(1,128)S(1)}, f32[16,1,128]{2,1,0:T(1,128)S(1)}, u32[]{:S(2)}, u32[]{:S(2)}) %collective-permute-start.10) | collective-permute-done | bytes 8224 | tf_op jit(solution)/shard_map/ppermute | solution.py:341
  90.5 0.9 collective-permute-done.9
  91.5 2.6 %multiply_convert_fusion = bf16[2048,1024]{1,0:T(8,128)(2,1)} fusion(bf16[2048,1024]{1,0:T(8,128)(2,1)S(1)} %copy-done.1, f32[1024]{0:T(1024)S(1)} %copy-done.6, f32[2048]{0:T(1024)S(1)} %bitcast.14), kind=kLoop, calls=%fused_computation | loop fusion | flops 8388608 | bytes 8400896 | tf_op jit(solution)/shard_map/convert_element_type | solution.py:357
  94.1 1.0 copy-done.9
  95.0 22.2 %attend.3 = bf16[2048,1024]{1,0:T(8,128)(2,1)} custom-call(s32[128]{0:T(128)} %reshape.29.owner_ref, s32[128]{0:T(128)} %reshape.30.block_ref, s32[16]{0:T(128)} %length_ref.3, bf16[2048,1024]{1,0:T(8,128)(2,1)} %q_ref.3, bf16[2048,256]{1,0:T(8,128)(2,1)} %get-tuple-element.30.new_k_ref, ...), custom_call_target="tpu_custom_call", output_to_operand_aliasing={{}: (10, {})} | custom-call | flops 30000001024 | bytes 20000000 | tf_op jit(solution)/shard_map/attend/pallas_call | solution.py:257
  (40 shorter events, 4.8 us)
Async XLA Ops:
  0.6 9.9 %copy-start.2 = (bf16[2048,2,128]{2,1,0:T(2,128)(2,1)S(1)}, bf16[2048,2,128]{2,1,0:T(2,128)(2,1)}, u32[]{:S(2)}) copy-start(bf16[2048,2,128]{2,1,0:T(2,128)(2,1)} %param.22) | copy-start | bytes 3145732
  0.6 17.3 %collective-permute-start = (bf16[4,1024,128]{2,1,0:T(8,128)(2,1)}, bf16[4,1024,128]{2,1,0:T(8,128)(2,1)}, u32[]{:S(2)}, u32[]{:S(2)}) collective-permute-start(bf16[4,1024,128]{2,1,0:T(8,128)(2,1)} %rest_0_), channel_id=1, source_target_pairs={{0,4},{4,0},{8,12},{12,8},{1,5},{5,1},{9,13},{13,9},{2,6},{6,2},{1... | collective-permute-start | bytes 3145736 | tf_op jit(solution)/shard_map/ppermute | solution.py:282
  1.2 26.7 %collective-permute-start.1 = (bf16[4,1024,128]{2,1,0:T(8,128)(2,1)}, bf16[4,1024,128]{2,1,0:T(8,128)(2,1)}, u32[]{:S(2)}, u32[]{:S(2)}) collective-permute-start(bf16[4,1024,128]{2,1,0:T(8,128)(2,1)} %rest_0_), channel_id=1, source_target_pairs={{0,8},{4,12},{8,0},{12,4},{1,9},{5,13},{9,1},{13,5},{2,10},{6,14},... | collective-permute-start | bytes 3145736 | tf_op jit(solution)/shard_map/ppermute | solution.py:282
  8.7 3.4 %copy-start = (bf16[2048,2,256]{2,1,0:T(2,128)(2,1)S(1)}, bf16[2048,2,256]{2,1,0:T(2,128)(2,1)}, u32[]{:S(2)}) copy-start(bf16[2048,2,256]{2,1,0:T(2,128)(2,1)} %param.17) | copy-start | bytes 6291460
  10.5 19.1 %copy-start.4 = (bf16[16,2,128,128]{3,2,1,0:T(8,128)(2,1)}, bf16[16,2,128,128]{3,2,1,0:T(8,128)(2,1)S(1)}, u32[]{:S(2)}) copy-start(bf16[16,2,128,128]{3,2,1,0:T(8,128)(2,1)S(1)} %get-tuple-element.43.rest_0_) | copy-start | bytes 3145732
  10.5 47.8 %copy-start.3 = (bf16[16,2,128,128]{3,2,1,0:T(8,128)(2,1)}, bf16[16,2,128,128]{3,2,1,0:T(8,128)(2,1)S(1)}, u32[]{:S(2)}) copy-start(bf16[16,2,128,128]{3,2,1,0:T(8,128)(2,1)S(1)} %get-tuple-element.46.rest_0_) | copy-start | bytes 3145732
  27.8 3.0 %collective-permute-start.4 = (bf16[4,1024,128]{2,1,0:T(8,128)(2,1)}, bf16[4,1024,128]{2,1,0:T(8,128)(2,1)}, u32[]{:S(2)}, u32[]{:S(2)}) collective-permute-start(bf16[4,1024,128]{2,1,0:T(8,128)(2,1)} %collective-permute-done.1.rest_2_), channel_id=1, source_target_pairs={{0,4},{4,0},{8,12},{12,8},{1,5},{5,1},{9,13},{13,9},{2,6},{6,2},{1... | collective-permute-start | bytes 3145736 | tf_op jit(solution)/shard_map/ppermute | solution.py:282
  27.8 27.5 %collective-permute-start.3 = (bf16[16,2,128,128]{3,2,1,0:T(8,128)(2,1)S(1)}, bf16[16,2,128,128]{3,2,1,0:T(8,128)(2,1)}, u32[]{:S(2)}, u32[]{:S(2)}) collective-permute-start(bf16[16,2,128,128]{3,2,1,0:T(8,128)(2,1)S(1)} %get-tuple-element.43.rest_0_), channel_id=1, source_target_pairs={{0,8},{4,12},{8,0},{12,4},{1,9},{5,13},{9,1},{13,5},{2,10},{6,14},... | collective-permute-start | bytes 3145736 | tf_op jit(solution)/shard_map/ppermute | solution.py:282
  29.6 25.8 %collective-permute-start.2 = (bf16[16,2,128,128]{3,2,1,0:T(8,128)(2,1)S(1)}, bf16[16,2,128,128]{3,2,1,0:T(8,128)(2,1)S(1)}, u32[]{:S(2)}, u32[]{:S(2)}) collective-permute-start(bf16[16,2,128,128]{3,2,1,0:T(8,128)(2,1)S(1)} %get-tuple-element.43.rest_0_), channel_id=1, source_target_pairs={{0,4},{4,0},{8,12},{12,8},{1,5},{5,1},{9,13},{13,9},{2,6},{6,2},{1... | collective-permute-start | bytes 3145736 | tf_op jit(solution)/shard_map/ppermute | solution.py:282
  55.4 1.0 copy-start.10
  56.4 25.7 %copy-start.5 = (f32[16,1,128]{2,1,0:T(1,128)S(1)}, f32[16,1,128]{2,1,0:T(1,128)}, u32[]{:S(2)}) copy-start(f32[16,1,128]{2,1,0:T(1,128)} %get-tuple-element.51) | copy-start | bytes 24580
  56.4 35.0 %copy-start.1 = (bf16[2048,1024]{1,0:T(8,128)(2,1)S(1)}, bf16[2048,1024]{1,0:T(8,128)(2,1)}, u32[]{:S(2)}) copy-start(bf16[2048,1024]{1,0:T(8,128)(2,1)} %get-tuple-element.50) | copy-start | bytes 12582916
  56.4 35.1 %copy-start.6 = (f32[1024]{0:T(1024)S(1)}, f32[1024]{0:T(1024)}, u32[]{:S(2)}) copy-start(f32[1024]{0:T(1024)} %param.26) | copy-start | bytes 12292
  56.4 3.0 %collective-permute-start.7 = (bf16[16,2,128,128]{3,2,1,0:T(8,128)(2,1)}, bf16[16,2,128,128]{3,2,1,0:T(8,128)(2,1)}, u32[]{:S(2)}, u32[]{:S(2)}) collective-permute-start(bf16[16,2,128,128]{3,2,1,0:T(8,128)(2,1)} %collective-permute-done.3.rest_2_), channel_id=1, source_target_pairs={{0,4},{4,0},{8,12},{12,8},{1,5},{5,1},{9,13},{13,9},{2,6},{6,2},{1... | collective-permute-start | bytes 3145736 | tf_op jit(solution)/shard_map/ppermute | solution.py:282
  56.5 25.4 %collective-permute-start.6 = (bf16[16,2,128,128]{3,2,1,0:T(8,128)(2,1)S(1)}, bf16[16,2,128,128]{3,2,1,0:T(8,128)(2,1)S(1)}, u32[]{:S(2)}, u32[]{:S(2)}) collective-permute-start(bf16[16,2,128,128]{3,2,1,0:T(8,128)(2,1)S(1)} %get-tuple-element.46.rest_0_), channel_id=1, source_target_pairs={{0,8},{4,12},{8,0},{12,4},{1,9},{5,13},{9,1},{13,5},{2,10},{6,14},... | collective-permute-start | bytes 3145736 | tf_op jit(solution)/shard_map/ppermute | solution.py:282
  58.3 23.7 %collective-permute-start.5 = (bf16[16,2,128,128]{3,2,1,0:T(8,128)(2,1)S(1)}, bf16[16,2,128,128]{3,2,1,0:T(8,128)(2,1)S(1)}, u32[]{:S(2)}, u32[]{:S(2)}) collective-permute-start(bf16[16,2,128,128]{3,2,1,0:T(8,128)(2,1)S(1)} %get-tuple-element.46.rest_0_), channel_id=1, source_target_pairs={{0,4},{4,0},{8,12},{12,8},{1,5},{5,1},{9,13},{13,9},{2,6},{6,2},{1... | collective-permute-start | bytes 3145736 | tf_op jit(solution)/shard_map/ppermute | solution.py:282
  82.0 12.1 %copy-start.7 = (bf16[16,2,128,128]{3,2,1,0:T(8,128)(2,1)}, bf16[16,2,128,128]{3,2,1,0:T(8,128)(2,1)S(1)}, u32[]{:S(2)}) copy-start(bf16[16,2,128,128]{3,2,1,0:T(8,128)(2,1)S(1)} %collective-permute-done.6.rest_2_) | copy-start | bytes 3145732
  82.0 12.1 %copy-start.8 = (bf16[16,2,128,128]{3,2,1,0:T(8,128)(2,1)}, bf16[16,2,128,128]{3,2,1,0:T(8,128)(2,1)S(1)}, u32[]{:S(2)}) copy-start(bf16[16,2,128,128]{3,2,1,0:T(8,128)(2,1)S(1)} %collective-permute-done.5.rest_1_) | copy-start | bytes 3145732
  82.0 12.1 %collective-permute-start.8 = (bf16[16,2,128,128]{3,2,1,0:T(8,128)(2,1)S(1)}, bf16[16,2,128,128]{3,2,1,0:T(8,128)(2,1)S(1)}, u32[]{:S(2)}, u32[]{:S(2)}) collective-permute-start(bf16[16,2,128,128]{3,2,1,0:T(8,128)(2,1)S(1)} %collective-permute-done.6.rest_2_), channel_id=1, source_target_pairs={{0,4},{4,0},{8,12},{12,8},{1,5},{5,1},{9,13},{13,9},{2,6},{6,2},{1... | collective-permute-start | bytes 3145736 | tf_op jit(solution)/shard_map/ppermute | solution.py:282
  82.1 5.2 %collective-permute-start.11 = (f32[16,1,128]{2,1,0:T(1,128)S(1)}, f32[16,1,128]{2,1,0:T(1,128)S(1)}, u32[]{:S(2)}, u32[]{:S(2)}) collective-permute-start(f32[16,1,128]{2,1,0:T(1,128)S(1)} %copy-done.5), channel_id=1, source_target_pairs={{0,3},{1,0},{2,1},{3,2},{4,7},{5,4},{6,5},{7,6},{8,11},{9,8},{10,9... | collective-permute-start | bytes 24584 | tf_op jit(solution)/shard_map/ppermute | solution.py:341
  86.0 4.5 %collective-permute-start.10 = (f32[16,1,128]{2,1,0:T(1,128)S(1)}, f32[16,1,128]{2,1,0:T(1,128)S(1)}, u32[]{:S(2)}, u32[]{:S(2)}) collective-permute-start(f32[16,1,128]{2,1,0:T(1,128)S(1)} %copy-done.5), channel_id=1, source_target_pairs={{0,2},{1,3},{2,0},{3,1},{4,6},{5,7},{6,4},{7,5},{8,10},{9,11},{10,... | collective-permute-start | bytes 24584 | tf_op jit(solution)/shard_map/ppermute | solution.py:341
  86.0 5.4 %collective-permute-start.9 = (f32[16,1,128]{2,1,0:T(1,128)S(1)}, f32[16,1,128]{2,1,0:T(1,128)S(1)}, u32[]{:S(2)}, u32[]{:S(2)}) collective-permute-start(f32[16,1,128]{2,1,0:T(1,128)S(1)} %copy-done.5), channel_id=1, source_target_pairs={{0,1},{1,2},{2,3},{3,0},{4,5},{5,6},{6,7},{7,4},{8,9},{9,10},{10,1... | collective-permute-start | bytes 24584 | tf_op jit(solution)/shard_map/ppermute | solution.py:341
  94.1 1.0 copy-start.9
